TPU v7x, 32 devices: a whole 2x2x4 slice. The times are simulated.
32 devices in a mesh: dp: 8 (over z, y), mp: 4 (over x, core).
Axes of the slice: x: 2, y: 2, z: 4, core: 2. Of those that a mesh axis runs over, the one named last changes fastest.
Arguments:
- query_states: bfloat16 [64, 32, 768], P('dp', None, 'mp'), may hold values from -6 to 6
- passage_states: bfloat16 [1024, 768, 128], P('dp', 'mp'), may hold values from -6 to 6
- projection: bfloat16 [768, 128], P('mp'), may hold values from -0.21875 to 0.21875
- candidates: int32 [64, 64], P(('dp', 'mp')), may hold values from 0 to 1023, as said below
Outputs:
- losses: float32 [64], P(('dp', 'mp'))
- weight_grad: float32 [768, 128], P('mp')
- query_grads: float32 [64, 32, 768], P('dp', None, 'mp')
- passage_grads: float32 [1024, 768, 128], P('dp', 'mp')
Inputs may be any that keep to these rules, and one draw needn't show every extreme that they name: `candidates`: the passage with id p is held by owner p // 32. Among the 128 entries of the 2 queries of one owner, at most 8 name passages of any one owner; in every draw some owners receive exactly 8 entries from every owner. A passage may be listed more than once, by one query or by several.
All inputs are finite; a program needn't handle non-finite values.
Results may differ from a plain program's by a relative error of at most 0.0064.
Values may be sent and summed in bfloat16 or wider, within the bound.
A program may use at most 192 MiB of HBM per device.

v0:
```python
import jax
import jax.numpy as jnp
from jax import lax
from jax.sharding import PartitionSpec as P

sharpness = 10.0
norm_eps = 1e-06


def unit_rows(pre):
    norm = jnp.sqrt(jnp.sum(pre * pre, axis=-1, keepdims=True) + norm_eps)
    return (pre / norm, norm)


def unit_back(grad, unit, norm):
    inner = jnp.sum(grad * unit, axis=-1, keepdims=True)
    return ((grad - unit * inner) / norm).astype(jnp.bfloat16)


def soft_maxsim(sim):
    expo = jnp.exp(sharpness * sim)
    total = jnp.sum(expo, axis=-1, keepdims=True)
    weights = expo / total
    score = jnp.sum(jnp.log(total[..., 0]), axis=-1) / sharpness
    return (score, weights)


def loss_parts(scores):
    expo = jnp.exp(scores)
    total = jnp.sum(expo, axis=-1, keepdims=True)
    prob = expo / total
    losses = jnp.log(total[..., 0]) - scores[..., 0]
    score_grad = prob.at[..., 0].add(-1.0)
    return (losses, score_grad)


def pick_rows(wanted_list, table_rows):
    held = table_rows.shape[0]
    picker = (wanted_list[:, None] == jnp.arange(held, dtype=jnp.int32)[None, :]).astype(
        jnp.bfloat16
    )
    flat = table_rows.reshape(held, -1)
    picked = jnp.dot(picker, flat, preferred_element_type=jnp.float32).astype(jnp.bfloat16)
    return picked.reshape((wanted_list.shape[0],) + table_rows.shape[1:])


def add_rows(wanted_list, terms, held):
    target = jnp.where(wanted_list < 0, held, wanted_list).astype(jnp.int32)
    summed = jnp.zeros((held,) + terms.shape[1:], jnp.float32)
    return summed.at[target].add(terms, mode="drop")


def on_device(query_states, passage_states, projection, candidates):
    f32 = jnp.float32
    owners = lax.axis_size(("dp", "mp"))
    groups = lax.axis_size("mp")
    query_rows, listed = candidates.shape
    qry_len = query_states.shape[1]
    emb_dim = projection.shape[1]
    passage_rows = passage_states.shape[0] // groups
    requests = query_rows * listed
    capacity = 2 * requests // owners
    sliced = query_states
    query_pre = lax.psum_scatter(
        jnp.einsum("nlh,he->nle", sliced, projection, preferred_element_type=f32),
        "mp",
        scatter_dimension=0,
        tiled=True,
    )
    sliced = passage_states
    passage_pre = lax.psum_scatter(
        jnp.einsum("nhl,he->nle", sliced, projection, preferred_element_type=f32),
        "mp",
        scatter_dimension=0,
        tiled=True,
    )
    query_unit, query_norm = unit_rows(query_pre)
    passage_unit, passage_norm = unit_rows(passage_pre)
    query_emb = query_unit.astype(jnp.bfloat16)
    passage_emb = passage_unit.astype(jnp.bfloat16)
    flat_ids = candidates.reshape(-1)
    owner_of = flat_ids // passage_rows
    local_of = flat_ids % passage_rows
    owner_table = (owner_of[:, None] == jnp.arange(owners, dtype=jnp.int32)[None, :]).astype(
        jnp.int32
    )
    within = jnp.sum(jnp.cumsum(owner_table, axis=0) * owner_table, axis=1) - 1
    slot_of = owner_of * capacity + within
    wanted = jnp.full((owners * capacity,), -1, jnp.int32).at[slot_of].set(local_of)
    wanted = wanted.reshape(owners, capacity)
    slot_total = owners * capacity
    query_copies = jnp.repeat(query_emb, listed, axis=0)
    query_send = (
        jnp.zeros((slot_total, qry_len, emb_dim), jnp.bfloat16).at[slot_of].set(query_copies)
    )
    asked, visitors = (
        lax.all_to_all(wanted, ("dp", "mp"), split_axis=0, concat_axis=0, tiled=True),
        lax.all_to_all(
            query_send.reshape(owners, capacity, qry_len, emb_dim),
            ("dp", "mp"),
            split_axis=0,
            concat_axis=0,
            tiled=True,
        ),
    )
    asked = asked.reshape(-1)
    visitors = visitors.reshape(slot_total, qry_len, emb_dim)
    rows_here = pick_rows(asked, passage_emb)
    sim = jnp.einsum("sie,sje->sij", visitors, rows_here, preferred_element_type=f32)
    slot_scores, weights = soft_maxsim(sim)
    score_back = lax.all_to_all(
        slot_scores.reshape(owners, capacity), ("dp", "mp"), split_axis=0, concat_axis=0, tiled=True
    )
    scores = score_back.reshape(-1)[slot_of].reshape(query_rows, listed)
    losses, score_grad = loss_parts(scores)
    grad_send = jnp.zeros((slot_total,), f32).at[slot_of].set(score_grad.reshape(-1))
    grad_here = lax.all_to_all(
        grad_send.reshape(owners, capacity), ("dp", "mp"), split_axis=0, concat_axis=0, tiled=True
    )
    sim_grad = (grad_here.reshape(-1)[:, None, None] * weights).astype(jnp.bfloat16)
    query_terms = jnp.einsum("sij,sje->sie", sim_grad, rows_here, preferred_element_type=f32)
    terms_back = lax.all_to_all(
        query_terms.reshape(owners, capacity, qry_len, emb_dim),
        ("dp", "mp"),
        split_axis=0,
        concat_axis=0,
        tiled=True,
    )
    mine = terms_back.reshape(slot_total, qry_len, emb_dim)[slot_of]
    query_emb_grad = jnp.sum(mine.reshape(query_rows, listed, qry_len, emb_dim), axis=1)
    passage_terms = jnp.einsum("sij,sie->sje", sim_grad, visitors, preferred_element_type=f32)
    passage_emb_grad = add_rows(asked, passage_terms, passage_rows)
    query_pre_grad = unit_back(query_emb_grad, query_unit, query_norm)
    passage_pre_grad = unit_back(passage_emb_grad, passage_unit, passage_norm)
    query_all, passage_all = (
        lax.all_gather(query_pre_grad, "mp", axis=0, tiled=True),
        lax.all_gather(passage_pre_grad, "mp", axis=0, tiled=True),
    )
    query_grads = jnp.einsum("nle,he->nlh", query_all, projection, preferred_element_type=f32)
    passage_grads = jnp.einsum("nle,he->nhl", passage_all, projection, preferred_element_type=f32)
    weight_part = jnp.einsum("nlh,nle->he", query_states, query_all, preferred_element_type=f32)
    weight_part = weight_part + jnp.einsum(
        "nhl,nle->he", passage_states, passage_all, preferred_element_type=f32
    )
    weight_grad = lax.psum(weight_part, "dp")
    return (losses, weight_grad, query_grads, passage_grads)


def solution(mesh):
    return jax.shard_map(
        on_device,
        mesh=mesh,
        in_specs=(P("dp", None, "mp"), P("dp", "mp", None), P("mp", None), P(("dp", "mp"), None)),
        out_specs=(P(("dp", "mp")), P("mp", None), P("dp", None, "mp"), P("dp", "mp", None)),
        check_vma=False,
    )
```

profile of v0, /device:TPU:0, one launch (start us, length us, event | category | flops | bytes accessed | tf_op | source)
XLA Modules:
  0.0 395.4 jit_solution(15327662484363087558)
XLA Ops:
  8.1 1.6 fusion.22
  9.8 8.6 %fusion.20 = f32[128,128,128]{2,1,0:T(8,128)} fusion(bf16[128,192,128]{2,1,0:T(8,128)(2,1)} %param.7, bf16[192,128]{1,0:T(8,128)(2,1)} %param.8), kind=kOutput, calls=%fused_computation.39 | convolution fusion | flops 805306368 | bytes 14729216 | tf_op jit(solution)/shard_map/nhl,he->nle/dot_general | solution.py:72
  19.7 1.0 scatter_custom_fusion.1
  21.4 7.3 %all-to-all-start.1 = ((s32[32,1,8]{2,1,0:T(1,128)}), s32[32,1,8]{2,1,0:T(1,128)S(1)}, u32[]{:S(2)}, u32[]{:S(2)}) async-start(s32[32,1,8]{2,1,0:T(1,128)} %bitcast.6), calls=%async_computation.2 | async-start | bytes 32768 | tf_op jit(solution)/shard_map/all_to_all | solution.py:97
  28.7 4.6 %reduce-scatter.3.cloned.1.call-done = f32[2,32,128]{2,1,0:T(8,128)} async-done(((f32[8,32,128]{2,1,0:T(8,128)}), f32[2,32,128]{2,1,0:T(8,128)}) %reduce-scatter.3.cloned.1.call-update) | async-done | bytes 32784 | tf_op jit(solution)/shard_map/reduce_scatter | solution.py:64
  35.5 4.5 %scatter_fusion = bf16[256,32,128]{2,1,0:T(8,128)(2,1)S(1)} fusion(bf16[256,32,128]{2,1,0:T(8,128)(2,1)S(1)} %broadcast_in_dim.13, s32[128]{0:T(128)S(1)} %fusion.25, bf16[128,32,128]{2,1,0:T(8,128)(2,1)S(1)} %bitcast.68), kind=kCustom, calls=%fused_computation.2 | custom fusion | bytes 3146240 | tf_op jit(solution)/shard_map/scatter | solution.py:94
  40.0 1.4 copy-done.3
  41.4 4.8 %all-to-all-start = ((bf16[32,8,32,128]{3,2,1,0:T(8,128)(2,1)}), bf16[32,8,32,128]{3,2,1,0:T(8,128)(2,1)S(1)}, u32[]{:S(2)}, u32[]{:S(2)}) async-start(bf16[32,8,32,128]{3,2,1,0:T(8,128)(2,1)} %bitcast.65), calls=%async_computation.1 | async-start | bytes 4194304 | tf_op jit(solution)/shard_map/all_to_all | solution.py:98
  47.5 70.8 %reduce-scatter.5.cloned.1.call-done = f32[32,128,128]{2,1,0:T(8,128)} async-done(((f32[128,128,128]{2,1,0:T(8,128)}), f32[32,128,128]{2,1,0:T(8,128)}) %reduce-scatter.5.cloned.1.call-update) | async-done | bytes 2097168 | tf_op jit(solution)/shard_map/reduce_scatter | solution.py:71
  118.4 2.2 multiply_reduce_fusion.1
  120.6 1.9 fusion.31
  122.5 5.8 %fusion.2 = bf16[32,8,128,128]{3,1,2,0:T(8,128)(2,1)} fusion(bf16[4,8,128,128]{3,2,1,0:T(8,128)(2,1)S(1)} %bitcast.66, s32[256]{0:T(256)S(1)} %eq.33), kind=kOutput, calls=%fused_computation.9 | convolution fusion | flops 272637952 | bytes 9438208 | tf_op jit(solution)/shard_map/dot_general | solution.py:43
  128.3 9.2 %copy.16 = bf16[32,8,128,128]{3,2,1,0:T(8,128)(2,1)} copy(bf16[32,8,128,128]{3,1,2,0:T(8,128)(2,1)} %fusion.2) | data formatting | bytes 16777216
  137.5 9.9 %fusion.3 = (f32[256,32]{1,0:T(8,128)S(1)}, f32[256,32,128]{2,1,0:T(8,128)}) fusion(bf16[256,32,128]{2,1,0:T(8,128)(2,1)S(1)} %bitcast.63, bf16[256,128,128]{2,1,0:T(8,128)(2,1)} %bitcast.61), kind=kOutput, calls=%fused_computation.13 | convolution fusion | flops 270524416 | bytes 14712832 | tf_op jit(solution)/shard_map/sie,sje->sij/dot_general | solution.py:109
  148.2 4.4 %all-to-all-start.2 = ((f32[32,1,8]{2,1,0:T(1,128)}), f32[32,1,8]{2,1,0:T(1,128)S(1)}, u32[]{:S(2)}, u32[]{:S(2)}) async-start(f32[32,1,8]{2,1,0:T(1,128)} %bitcast.7), calls=%async_computation.4 | async-start | bytes 32768 | tf_op jit(solution)/shard_map/all_to_all | solution.py:111
  153.4 6.3 %all-to-all-done.2 = f32[32,1,8]{2,1,0:T(1,128)S(1)} async-done(((f32[32,1,8]{2,1,0:T(1,128)}), f32[32,1,8]{2,1,0:T(1,128)S(1)}, u32[]{:S(2)}, u32[]{:S(2)}) %all-to-all-start.2) | async-done | bytes 1056 | tf_op jit(solution)/shard_map/all_to_all | solution.py:111
  161.0 1.3 gather_fusion
  163.3 1.0 scatter_custom_fusion.2
  165.0 2.8 all-to-all-start.3
  167.8 6.8 %all-to-all-done.3 = f32[32,1,8]{2,1,0:T(1,128)S(1)} async-done(((f32[32,1,8]{2,1,0:T(1,128)}), f32[32,1,8]{2,1,0:T(1,128)S(1)}, u32[]{:S(2)}, u32[]{:S(2)}) %all-to-all-start.3) | async-done | bytes 1056 | tf_op jit(solution)/shard_map/all_to_all | solution.py:117
  175.4 7.4 %fusion.33 = f32[256,32,128]{2,1,0:T(8,128)} fusion(bf16[256,128,128]{2,1,0:T(8,128)(2,1)} %bitcast.62, f32[256,32,128]{2,1,0:T(8,128)} %get-tuple-element.19, f32[256,32]{1,0:T(8,128)S(1)} %get-tuple-element.18, f32[256]{0:T(256)S(1)} %mul.67), kind=kOutput, calls=%fused_computation.78 | convolution fusion | flops 272629760 | bytes 16811008 | tf_op jit(solution)/shard_map/sij,sje->sie/dot_general | solution.py:121
  182.8 9.0 %fusion.32 = f32[256,128,128]{2,1,0:T(8,128)} fusion(bf16[256,32,128]{2,1,0:T(8,128)(2,1)S(1)} %bitcast.64, f32[256,32,128]{2,1,0:T(8,128)S(1)} %copy-done.2, f32[256,32]{1,0:T(8,128)S(1)} %get-tuple-element.18, f32[256]{0:T(256)S(1)} %mul.67), kind=kOutput, calls=%fused_computation.77 | convolution fusion | flops 272629760 | bytes 23102464 | tf_op jit(solution)/shard_map/sij,sie->sje/dot_general | solution.py:131
  191.8 3.6 all-to-all-start.4
  195.7 33.1 %scatter_fusion.1 = f32[32,128,128]{2,1,0:T(8,128)S(1)} fusion(f32[32,128,128]{2,1,0:T(8,128)S(1)} %broadcast_in_dim.17, s32[256]{0:T(256)S(1)} %bitcast.70, f32[256,128,128]{2,1,0:T(8,128)} %fusion.32), kind=kCustom, calls=%fused_computation.5 | custom fusion | flops 4194304 | bytes 50332672 | tf_op jit(solution)/shard_map/scatter-add | solution.py:50
  228.8 25.6 %divide_convert_fusion = bf16[32,128,128]{2,1,0:T(8,128)(2,1)} fusion(f32[32,128,128]{2,1,0:T(8,128)S(1)} %scatter_fusion.1, f32[32,128]{1,0:T(8,128)S(1)} %add_sqrt_fusion, f32[32,128,128]{2,1,0:T(8,128)} %reduce-scatter.5.cloned.1.call-done), kind=kOutput, calls=%fused_computation.15 | output fusion | flops 3674239 | bytes 5259264 | tf_op jit(solution)/shard_map/mul | solution.py:17
  255.1 40.7 %all-gather.2.cloned.1.call-done = bf16[128,128,128]{2,1,0:T(8,128)(2,1)} async-done(((bf16[32,128,128]{2,1,0:T(8,128)(2,1)}), bf16[128,128,128]{2,1,0:T(8,128)(2,1)}) %all-gather.2.cloned.1.call-update) | async-done | bytes 4194320 | tf_op jit(solution)/shard_map/all_gather | solution.py:137
  295.8 5.9 %convolution_bitcast_fusion.1 = f32[128,192]{0,1:T(8,128)S(1)} fusion(bf16[128,192,128]{2,1,0:T(8,128)(2,1)} %param.7, bf16[128,128,128]{2,1,0:T(8,128)(2,1)} %all-gather.2.cloned.1.call-done), kind=kOutput, calls=%fused_computation.19 | convolution fusion | flops 805306368 | bytes 10584064 | tf_op jit(solution)/shard_map/nhl,nle->he/dot_general | solution.py:142
  301.7 6.6 %convolution_bitcast_fusion = f32[128,192,128]{2,1,0:T(8,128)} fusion(bf16[128,128,128]{2,1,0:T(8,128)(2,1)S(1)} %copy-done.1, bf16[192,128]{1,0:T(8,128)(2,1)S(1)} %copy-done.4), kind=kOutput, calls=%fused_computation.10 | convolution fusion | flops 805306368 | bytes 16826368 | tf_op jit(solution)/shard_map/nle,he->nhl/dot_general | solution.py:140
  308.3 2.9 gather_fusion.1
  311.5 5.2 %all_gather.6 = bf16[8,32,128]{2,1,0:T(8,128)(2,1)S(1)} all-gather(bf16[2,32,128]{2,1,0:T(8,128)(2,1)S(1)} %fusion.12), channel_id=1, replica_groups=mesh['dp'=8,'mp'=4] {'mp'}, dimensions={0}, use_global_device_ids=true | all-gather | bytes 81920 | tf_op jit(solution)/shard_map/all_gather | solution.py:136
  318.6 68.7 %all-reduce.2.cloned.1.call-done = f32[192,128]{1,0:T(8,128)} async-done(((f32[192,128]{1,0:T(8,128)}), f32[192,128]{1,0:T(8,128)}) %all-reduce.2.cloned.1.call-update) | async-done | bytes 98320 | tf_op jit(solution)/shard_map/psum | solution.py:145
  387.3 1.5 copy.25
  (67 shorter events, 14.8 us)
Async XLA Ops:
  7.2 0.9 copy-start
  7.2 26.2 %reduce-scatter.3.cloned.1.call-start = ((), (), s32[]{:S(2)}) async-start(), calls=%async_computation.7 | async-start | bytes 163840 | tf_op jit(solution)/shard_map/reduce_scatter | solution.py:64
  9.7 108.6 %reduce-scatter.5.cloned.1.call-start = ((), (), s32[]{:S(2)}) async-start(), calls=%async_computation.8 | async-start | bytes 10485760 | tf_op jit(solution)/shard_map/reduce_scatter | solution.py:71
  18.4 0.7 copy-start.6
  21.4 18.6 %all-to-all-start.1 = ((s32[32,1,8]{2,1,0:T(1,128)}), s32[32,1,8]{2,1,0:T(1,128)S(1)}, u32[]{:S(2)}, u32[]{:S(2)}) async-start(s32[32,1,8]{2,1,0:T(1,128)} %bitcast.6), calls=%async_computation.2 | async-start | bytes 32768 | tf_op jit(solution)/shard_map/all_to_all | solution.py:97
  40.0 1.4 copy-start.3
  41.4 96.1 %all-to-all-start = ((bf16[32,8,32,128]{3,2,1,0:T(8,128)(2,1)}), bf16[32,8,32,128]{3,2,1,0:T(8,128)(2,1)S(1)}, u32[]{:S(2)}, u32[]{:S(2)}) async-start(bf16[32,8,32,128]{3,2,1,0:T(8,128)(2,1)} %bitcast.65), calls=%async_computation.1 | async-start | bytes 4194304 | tf_op jit(solution)/shard_map/all_to_all | solution.py:98
  148.2 11.5 %all-to-all-start.2 = ((f32[32,1,8]{2,1,0:T(1,128)}), f32[32,1,8]{2,1,0:T(1,128)S(1)}, u32[]{:S(2)}, u32[]{:S(2)}) async-start(f32[32,1,8]{2,1,0:T(1,128)} %bitcast.7), calls=%async_computation.4 | async-start | bytes 32768 | tf_op jit(solution)/shard_map/all_to_all | solution.py:111
  165.0 9.6 %all-to-all-start.3 = ((f32[32,1,8]{2,1,0:T(1,128)}), f32[32,1,8]{2,1,0:T(1,128)S(1)}, u32[]{:S(2)}, u32[]{:S(2)}) async-start(f32[32,1,8]{2,1,0:T(1,128)} %bitcast.8), calls=%async_computation.5 | async-start | bytes 32768 | tf_op jit(solution)/shard_map/all_to_all | solution.py:117
  175.4 7.4 %copy-start.2 = (f32[256,32,128]{2,1,0:T(8,128)S(1)}, f32[256,32,128]{2,1,0:T(8,128)}, u32[]{:S(2)}) copy-start(f32[256,32,128]{2,1,0:T(8,128)} %get-tuple-element.19) | copy-start | bytes 12582916
  191.8 116.5 %all-to-all-start.4 = ((f32[32,8,32,128]{3,2,1,0:T(8,128)}), f32[32,8,32,128]{3,2,1,0:T(8,128)}, u32[]{:S(2)}, u32[]{:S(2)}) async-start(f32[32,8,32,128]{3,2,1,0:T(8,128)} %bitcast.67), calls=%async_computation.6 | async-start | bytes 8388608 | tf_op jit(solution)/shard_map/all_to_all | solution.py:122
  195.4 100.4 %all-gather.2.cloned.1.call-start = ((), (), s32[]{:S(2)}) async-start(), calls=%async_computation.9 | async-start | bytes 5242880 | tf_op jit(solution)/shard_map/all_gather | solution.py:137
  254.4 132.9 %all-reduce.2.cloned.1.call-start = ((), (), s32[]{:S(2)}) async-start(), calls=%async_computation.10 | async-start | bytes 196608 | tf_op jit(solution)/shard_map/psum | solution.py:145
  255.1 46.7 %copy-start.4 = (bf16[192,128]{1,0:T(8,128)(2,1)S(1)}, bf16[192,128]{1,0:T(8,128)(2,1)}, u32[]{:S(2)}) copy-start(bf16[192,128]{1,0:T(8,128)(2,1)} %param.8) | copy-start | bytes 147460
  295.8 6.0 %copy-start.1 = (bf16[128,128,128]{2,1,0:T(8,128)(2,1)S(1)}, bf16[128,128,128]{2,1,0:T(8,128)(2,1)}, u32[]{:S(2)}) copy-start(bf16[128,128,128]{2,1,0:T(8,128)(2,1)} %all-gather.2.cloned.1.call-done) | copy-start | bytes 12582916
  308.3 3.0 copy-start.5
Sparse Core Ops, SparseCore 0:
  11.0 22.2 reduce-scatter.2
  36.7 81.6 reduce-scatter.4
  254.5 41.2 all-gather.1
  317.8 69.4 all-reduce.1
where the time goes:
time: 397 us; the launch traced here: 395 us
  waiting for transfers between devices  198 us (50%)
  other arithmetic  69.5 us (18%)
  matrix products  56.6 us (14%)
  local copies, waits for them, and re-layouts  28.8 us (7%)
  starting transfers between devices  23 us (6%)
  between operations  14.1 us (4%)
  blocking collectives  5.24 us (1%)
    reduce_scatter x1, waiting for transfers between devices, on_device(): lax.psum_scatter(jnp.einsum('nhl,he->nle', sliced, projection, preferred_...  70.8 us
    psum x1, waiting for transfers between devices, on_device(): weight_grad = lax.psum(weight_part, 'dp')  68.7 us
    all_gather x1, waiting for transfers between devices, on_device(): lax.all_gather(passage_pre_grad, 'mp', axis=0, tiled=True)  40.7 us
    scatter-add x1, other arithmetic, add_rows(): return summed.at[target].add(terms, mode='drop')  33.1 us
    mul x2, other arithmetic, unit_back(): return ((grad - unit * inner) / norm).astype(jnp.bfloat16)  25.8 us
    unnamed x16, local copies, waits for them, and re-layouts  13.6 us
    dot_general x1, matrix products, on_device(): jnp.einsum('sie,sje->sij', visitors, rows_here, preferred_element_type=f32)  9.9 us
    dot_general x1, matrix products, on_device(): jnp.einsum('sij,sie->sje', sim_grad, visitors, preferred_element_type=f32)  8.99 us
  transfers between devices with their start and end apart: 9, of which 6 were waited for; matrix products, arithmetic and copies ran while one was open for 28% of the time, Pallas kernels for 0%

commit v1 on v0

v1 whole, which is shorter than its diff:
```python
import jax
import jax.numpy as jnp
from jax import lax
from jax.experimental import pallas as pl
from jax.experimental.pallas import tpu as pltpu
from jax.sharding import PartitionSpec as P

sharpness = 10.0
norm_eps = 1e-06
BATCH = 8
VMEM_LIMIT = 56 * 1024 * 1024


def unit_rows(pre):
    norm = jnp.sqrt(jnp.sum(pre * pre, axis=-1, keepdims=True) + norm_eps)
    return (pre / norm, norm)


def unit_back(grad, unit, norm):
    inner = jnp.sum(grad * unit, axis=-1, keepdims=True)
    return ((grad - unit * inner) / norm).astype(jnp.bfloat16)


def score_kernel(local_ref, query_ref, pre_ref, visitors_ref, emb_ref, weights_ref, scores_ref):
    def embed(p, carry):
        unit, _ = unit_rows(pre_ref[p])
        emb_ref[p] = unit.astype(jnp.bfloat16)
        return carry

    lax.fori_loop(0, pre_ref.shape[0], embed, 0)

    def slots(b, carry):
        for u in range(BATCH):
            s = b * BATCH + u
            sim = lax.dot_general(
                visitors_ref[query_ref[s]],
                emb_ref[local_ref[s]],
                (((1,), (1,)), ((), ())),
                preferred_element_type=jnp.float32,
            )
            expo = jnp.exp(sharpness * sim)
            total = jnp.sum(expo, axis=-1, keepdims=True)
            weights_ref[s] = expo / total
            score = jnp.sum(jnp.log(total), axis=0, keepdims=True) / sharpness
            scores_ref[s] = jnp.broadcast_to(score, scores_ref.shape[1:])
        return carry

    lax.fori_loop(0, weights_ref.shape[0] // BATCH, slots, 0)


def grad_kernel(
    local_ref, query_ref, grad_ref, pre_ref, emb_ref, visitors_ref, weights_ref,
    query_grad_ref, pre_grad_ref, query_sum, passage_sum
):
    query_sum[...] = jnp.zeros_like(query_sum)
    passage_sum[...] = jnp.zeros_like(passage_sum)

    def slots(b, carry):
        found = []
        for u in range(BATCH):
            s = b * BATCH + u
            p = local_ref[s]
            q = query_ref[s]
            sim_grad = (grad_ref[s] * weights_ref[s]).astype(jnp.bfloat16)
            query_term = jnp.dot(sim_grad, emb_ref[p], preferred_element_type=jnp.float32)
            passage_term = lax.dot_general(
                sim_grad,
                visitors_ref[q],
                (((0,), (0,)), ((), ())),
                preferred_element_type=jnp.float32,
            )
            found.append((p, q, query_term, passage_term))
        for p, q, query_term, passage_term in found:
            query_sum[q] += query_term
            passage_sum[p] += passage_term
        return carry

    lax.fori_loop(0, weights_ref.shape[0] // BATCH, slots, 0)
    query_grad_ref[...] = query_sum[...].astype(jnp.bfloat16)

    def back(p, carry):
        unit, norm = unit_rows(pre_ref[p])
        pre_grad_ref[p] = unit_back(passage_sum[p], unit, norm)
        return carry

    lax.fori_loop(0, pre_ref.shape[0], back, 0)


def swap(array, bit, groups):
    return lax.ppermute(array, "mp", [(i, i ^ bit) for i in range(groups)])


def reduce_mp(states, project, groups, dtype):
    f32 = jnp.float32
    me = lax.axis_index("mp")
    rows = states.shape[0] // groups

    def block(index):
        return project(lax.dynamic_slice_in_dim(states, index * rows, rows, 0))

    if groups != 4:
        return lax.psum_scatter(project(states), "mp", scatter_dimension=0, tiled=True)
    far_out = swap(block(me ^ 3).astype(dtype), 1, groups)
    near_out = swap(block(me ^ 1).astype(dtype), 1, groups)
    far = block(me ^ 2) + far_out.astype(f32)
    far_in = swap(far.astype(dtype), 2, groups)
    return (block(me) + near_out.astype(f32)) + far_in.astype(f32)


def gather_mp(mine, groups):
    if groups != 4:
        return lax.all_gather(mine, "mp", axis=0, tiled=True)
    me = lax.axis_index("mp")
    far = swap(mine, 2, groups)
    near = swap(mine, 1, groups)
    far_near = swap(far, 1, groups)
    odd = (me & 1) == 1
    here = jnp.concatenate([jnp.where(odd, near, mine), jnp.where(odd, mine, near)])
    there = jnp.concatenate([jnp.where(odd, far_near, far), jnp.where(odd, far, far_near)])
    high = (me & 2) == 2
    return jnp.concatenate([jnp.where(high, there, here), jnp.where(high, here, there)])


def exchange(array, axes):
    return lax.all_to_all(array, axes, split_axis=0, concat_axis=0, tiled=True)


def spread(array, axes, size):
    return exchange(jnp.broadcast_to(array[None], (size,) + array.shape), axes)


def on_device(query_states, passage_states, projection, candidates):
    f32 = jnp.float32
    both = ("dp", "mp")
    owners = lax.axis_size(both)
    groups = lax.axis_size("mp")
    replicas = lax.axis_size("dp")
    me = lax.axis_index(both)
    query_rows, listed = candidates.shape
    qry_len = query_states.shape[1]
    emb_dim = projection.shape[1]
    psg_len = passage_states.shape[2]
    passage_rows = passage_states.shape[0] // groups
    requests = query_rows * listed
    capacity = 2 * requests // owners
    slot_total = owners * capacity
    queries = owners * query_rows

    listings = spread(candidates, both, owners).reshape(owners, requests)
    query_pre = reduce_mp(
        query_states,
        lambda s: jnp.einsum("nlh,he->nle", s, projection, preferred_element_type=f32),
        groups,
        f32,
    )
    query_unit, query_norm = unit_rows(query_pre)
    visitors = spread(query_unit.astype(jnp.bfloat16), both, owners)
    visitors = visitors.reshape(queries, qry_len, emb_dim)
    passage_pre = reduce_mp(
        passage_states,
        lambda s: jnp.einsum("nhl,he->nle", s, projection, preferred_element_type=f32),
        groups,
        jnp.bfloat16,
    )

    held = (listings // passage_rows) == me
    within = jnp.cumsum(held.astype(jnp.int32), axis=1) - 1
    chosen = held[:, None, :] & (
        within[:, None, :] == jnp.arange(capacity, dtype=jnp.int32)[None, :, None]
    )
    entry = jnp.arange(requests, dtype=jnp.int32)
    valid = jnp.any(chosen, axis=-1).reshape(-1)
    entry_of = jnp.sum(jnp.where(chosen, entry[None, None, :], 0), axis=-1)
    local_of = jnp.sum(jnp.where(chosen, (listings % passage_rows)[:, None, :], 0), axis=-1)
    source = jnp.arange(owners, dtype=jnp.int32)[:, None]
    query_of = (source * query_rows + entry_of // listed).reshape(-1)
    local_of = local_of.reshape(-1)
    first = valid & ((entry_of % listed).reshape(-1) == 0)

    smem = pl.BlockSpec(memory_space=pltpu.SMEM)
    vmem = pl.BlockSpec(memory_space=pltpu.VMEM)
    params = pltpu.CompilerParams(vmem_limit_bytes=VMEM_LIMIT)
    block_shape = (passage_rows, psg_len, emb_dim)
    passage_emb, weights, slot_scores = pl.pallas_call(
        score_kernel,
        out_shape=(
            jax.ShapeDtypeStruct(block_shape, jnp.bfloat16),
            jax.ShapeDtypeStruct((slot_total, qry_len, psg_len), f32),
            jax.ShapeDtypeStruct((slot_total, 1, 128), f32),
        ),
        in_specs=[smem, smem, vmem, vmem],
        out_specs=(vmem, vmem, vmem),
        compiler_params=params,
    )(local_of, query_of, passage_pre, visitors)
    slot_scores = slot_scores[:, 0, 0]

    mine = valid[None, :] & (query_of[None, :] == jnp.arange(queries, dtype=jnp.int32)[:, None])
    slot_expo = jnp.exp(slot_scores)
    part_total = jnp.sum(jnp.where(mine, slot_expo[None, :], 0.0), axis=1)
    part_first = jnp.sum(jnp.where(mine & first[None, :], slot_scores[None, :], 0.0), axis=1)
    sums = jnp.sum(spread(jnp.stack([part_total, part_first]), both, owners).reshape(owners, 2, queries), axis=0)
    total_of = jnp.sum(jnp.where(mine, sums[0][:, None], 0.0), axis=0)
    slot_grad = jnp.where(
        valid, slot_expo / jnp.where(valid, total_of, 1.0) - first.astype(f32), 0.0
    )
    losses = lax.dynamic_slice_in_dim(jnp.log(sums[0]) - sums[1], me * query_rows, query_rows)

    query_terms, passage_pre_grad = pl.pallas_call(
        grad_kernel,
        out_shape=(
            jax.ShapeDtypeStruct((queries, qry_len, emb_dim), jnp.bfloat16),
            jax.ShapeDtypeStruct(block_shape, jnp.bfloat16),
        ),
        in_specs=[smem, smem, smem, vmem, vmem, vmem, vmem],
        out_specs=(vmem, vmem),
        scratch_shapes=[
            pltpu.VMEM((queries, qry_len, emb_dim), f32),
            pltpu.VMEM(block_shape, f32),
        ],
        compiler_params=params,
    )(local_of, query_of, slot_grad, passage_pre, passage_emb, visitors, weights)

    terms_back = exchange(query_terms.reshape(owners, query_rows, qry_len, emb_dim), both)
    query_emb_grad = jnp.sum(
        terms_back.reshape(owners, query_rows, qry_len, emb_dim).astype(f32), axis=0
    )
    query_pre_grad = unit_back(query_emb_grad, query_unit, query_norm)
    passage_all = gather_mp(passage_pre_grad, groups)
    query_all = gather_mp(query_pre_grad, groups)
    weight_part = jnp.einsum("nlh,nle->he", query_states, query_all, preferred_element_type=f32)
    weight_part = weight_part + jnp.einsum(
        "nhl,nle->he", passage_states, passage_all, preferred_element_type=f32
    )
    height = weight_part.shape[0] // replicas
    pieces = exchange(weight_part.reshape(replicas, height, emb_dim), "dp")
    piece = jnp.sum(pieces.reshape(replicas, height, emb_dim), axis=0)
    weight_grad = spread(piece, "dp", replicas).reshape(weight_part.shape)
    query_grads = jnp.einsum("nle,he->nlh", query_all, projection, preferred_element_type=f32)
    passage_grads = jnp.einsum("nle,he->nhl", passage_all, projection, preferred_element_type=f32)
    return (losses, weight_grad, query_grads, passage_grads)


def solution(mesh):
    return jax.shard_map(
        on_device,
        mesh=mesh,
        in_specs=(P("dp", None, "mp"), P("dp", "mp", None), P("mp", None), P(("dp", "mp"), None)),
        out_specs=(P(("dp", "mp")), P("mp", None), P("dp", None, "mp"), P("dp", "mp", None)),
        check_vma=False,
    )
```

time: 397 us -> 189 us (0.48)
  waiting for transfers between devices: 198 us -> 56.4 us
  other arithmetic: 69.5 us -> 10.6 us
  Pallas kernels: 0 us -> 38.5 us
  matrix products: 56.6 us -> 24.9 us
  local copies, waits for them, and re-layouts: 28.8 us -> 12.4 us
  between operations: 14.1 us -> 0.97 us
  starting transfers between devices: 23 us -> 31.9 us
  blocking collectives: 5.24 us -> 12.7 us
    reduce_scatter x2 -> x0, waiting for transfers between devices: 75.5 us -> none  [the longest x1 70.8 us: on_device(): lax.psum_scatter(jnp.einsum('nhl,he->nle', sliced, projection, preferred_...]
    psum x1 -> x0, waiting for transfers between devices: 68.7 us -> none  [on_device(): weight_grad = lax.psum(weight_part, 'dp')]
    all_gather x1 -> x0, waiting for transfers between devices: 40.7 us -> none  [on_device(): lax.all_gather(passage_pre_grad, 'mp', axis=0, tiled=True)]
    pallas_call x0 -> x2, Pallas kernels: none -> 38.5 us  [the longest x1 19.8 us: on_device(): pl.pallas_call(grad_kernel, out_shape=(jax.ShapeDtypeStruct((queries, qry...]
    ppermute x0 -> x12, waiting for transfers between devices: none -> 36.3 us  [swap(): return lax.ppermute(array, 'mp', [(i, i ^ bit) for i in range(groups)])]
    scatter-add x1 -> x0, other arithmetic: 33.1 us -> none  [add_rows(): return summed.at[target].add(terms, mode='drop')]
    dot_general x6 -> x8, matrix products: 42.3 us -> 13.2 us  [the longest x4 11 us: on_device(): jnp.einsum('nhl,he->nle', s, projection, preferred_element_type=f32)]
    mul x2 -> x1, other arithmetic: 25.8 us -> 0.18 us  [unit_back(): return ((grad - unit * inner) / norm).astype(jnp.bfloat16)]
  transfers between devices with their start and end apart: 9 -> 17, of which waited for: 6 -> 6; matrix products, arithmetic and copies ran while one was open for 28% -> 18% of each run, Pallas kernels for 0% -> 0%
where the time goes in v1:
time: 189 us; the launch traced here: 188 us
  waiting for transfers between devices  56.4 us (30%)
  Pallas kernels  38.5 us (20%)
  starting transfers between devices  31.9 us (17%)
  matrix products  24.9 us (13%)
  blocking collectives  12.7 us (7%)
  local copies, waits for them, and re-layouts  12.4 us (7%)
  other arithmetic  10.6 us (6%)
    ppermute x12, waiting for transfers between devices, swap(): return lax.ppermute(array, 'mp', [(i, i ^ bit) for i in range(groups)])  36.3 us
    all_to_all x5, starting transfers between devices, exchange(): return lax.all_to_all(array, axes, split_axis=0, concat_axis=0, tiled=True)  23.6 us
    all_to_all x5, waiting for transfers between devices, exchange(): return lax.all_to_all(array, axes, split_axis=0, concat_axis=0, tiled=True)  20.1 us
    pallas_call x1, Pallas kernels, on_device(): pl.pallas_call(grad_kernel, out_shape=(jax.ShapeDtypeStruct((queries, qry...  19.8 us
    pallas_call x1, Pallas kernels, on_device(): pl.pallas_call(score_kernel, out_shape=(jax.ShapeDtypeStruct(block_shape,...  18.7 us
    all_to_all x1, blocking collectives, exchange(): return lax.all_to_all(array, axes, split_axis=0, concat_axis=0, tiled=True)  12.7 us
    dot_general x4, matrix products, on_device(): jnp.einsum('nhl,he->nle', s, projection, preferred_element_type=f32)  11 us
    ppermute x12, starting transfers between devices, swap(): return lax.ppermute(array, 'mp', [(i, i ^ bit) for i in range(groups)])  8.23 us
  transfers between devices with their start and end apart: 17, of which 6 were waited for; matrix products, arithmetic and copies ran while one was open for 18% of the time, Pallas kernels for 0%

profile of v1, /device:TPU:0, one launch (start us, length us, event | category | flops | bytes accessed | tf_op | source)
XLA Modules:
  0.0 188.3 jit_solution(4077463303066605997)
XLA Ops:
  2.1 7.3 %all-to-all-start = ((s32[32,1,128]{2,1,0:T(1,128)}), s32[32,1,128]{2,1,0:T(1,128)S(1)}, u32[]{:S(2)}, u32[]{:S(2)}) async-start(s32[32,1,128]{2,1,0:T(1,128)} %reshape.214), calls=%async_computation | async-start | bytes 32768 | tf_op jit(solution)/shard_map/all_to_all | solution.py:125
  9.4 0.9 fusion.32
  10.6 0.9 fusion.35
  11.8 2.2 %fusion.15 = bf16[32,128,128]{2,1,0:T(8,128)(2,1)S(1)} fusion(bf16[128,192,128]{2,1,0:T(8,128)(2,1)} %param.5, s32[]{:T(128)S(6)} %select_n.170, bf16[192,128]{1,0:T(8,128)(2,1)} %param.6), kind=kOutput, calls=%fused_computation.19 | convolution fusion | flops 201850880 | bytes 2670596 | tf_op jit(solution)/shard_map/nhl,he->nle/dot_general | solution.py:161
  14.3 3.2 %fusion.10 = bf16[32,128,128]{2,1,0:T(8,128)(2,1)} fusion(bf16[128,192,128]{2,1,0:T(8,128)(2,1)} %param.5, s32[]{:T(128)S(6)} %select_n.168, bf16[192,128]{1,0:T(8,128)(2,1)S(1)} %copy-done.2), kind=kOutput, calls=%fused_computation.18 | convolution fusion | flops 201850880 | bytes 2670596 | tf_op jit(solution)/shard_map/nhl,he->nle/dot_general | solution.py:161
  17.8 2.2 %fusion.8 = f32[32,128,128]{2,1,0:T(8,128)S(1)} fusion(bf16[128,192,128]{2,1,0:T(8,128)(2,1)} %param.5, s32[]{:T(128)S(6)} %select_n.167, bf16[192,128]{1,0:T(8,128)(2,1)S(1)} %copy-done.2), kind=kOutput, calls=%fused_computation.16 | convolution fusion | flops 201326592 | bytes 3719172 | tf_op jit(solution)/shard_map/nhl,he->nle/dot_general | solution.py:161
  22.0 1.8 collective-permute-start.5
  23.8 2.1 %collective-permute-done.5 = f32[2,32,128]{2,1,0:T(8,128)S(1)} collective-permute-done((f32[2,32,128]{2,1,0:T(8,128)S(1)}, f32[2,32,128]{2,1,0:T(8,128)S(1)}, u32[]{:S(2)}, u32[]{:S(2)}) %collective-permute-start.5) | collective-permute-done | bytes 32800 | tf_op jit(solution)/shard_map/ppermute | solution.py:90
  26.2 3.5 %add_convert_fusion = bf16[32,128,128]{2,1,0:T(8,128)(2,1)} fusion(bf16[32,128,128]{2,1,0:T(8,128)(2,1)} %collective-permute-done.1, bf16[128,192,128]{2,1,0:T(8,128)(2,1)} %param.5, s32[]{:T(128)S(6)} %select_n.169, bf16[192,128]{1,0:T(8,128)(2,1)S(1)} %copy-done.2), kind=kOutput, calls=%fused_computation.7 | convolution fusion | flops 202899456 | bytes 3719172 | tf_op jit(solution)/shard_map/nhl,he->nle/dot_general | solution.py:161
  29.6 1.8 collective-permute-start.2
  31.5 0.9 broadcast_in_dim.96
  32.4 4.6 %all-to-all-start.1 = ((bf16[32,2,32,128]{3,2,1,0:T(8,128)(2,1)}), bf16[32,2,32,128]{3,2,1,0:T(8,128)(2,1)S(1)}, u32[]{:S(2)}, u32[]{:S(2)}) async-start(bf16[32,2,32,128]{3,2,1,0:T(8,128)(2,1)} %broadcast_in_dim.96), calls=%async_computation.1 | async-start | bytes 1048576 | tf_op jit(solution)/shard_map/all_to_all | solution.py:125
  37.8 1.2 select_reduce_fusion.1
  40.3 18.7 %collective-permute-done.2 = bf16[32,128,128]{2,1,0:T(8,128)(2,1)} collective-permute-done((bf16[32,128,128]{2,1,0:T(8,128)(2,1)}, bf16[32,128,128]{2,1,0:T(8,128)(2,1)}, u32[]{:S(2)}, u32[]{:S(2)}) %collective-permute-start.2) | collective-permute-done | bytes 1048608 | tf_op jit(solution)/shard_map/ppermute | solution.py:90
  59.0 3.3 %convert_add_fusion.pre_ref = f32[32,128,128]{2,1,0:T(8,128)} fusion(bf16[32,128,128]{2,1,0:T(8,128)(2,1)} %collective-permute-done.2, f32[32,128,128]{2,1,0:T(8,128)S(1)} %fusion.8, bf16[32,128,128]{2,1,0:T(8,128)(2,1)} %collective-permute-done), kind=kLoop, calls=%fused_computation.6 | loop fusion | flops 2097152 | bytes 6291456 | tf_op jit(solution)/shard_map/add | solution.py:107
  63.1 18.7 %shard_map.75 = (bf16[32,128,128]{2,1,0:T(8,128)(2,1)}, f32[256,32,128]{2,1,0:T(8,128)}, f32[256,1,128]{2,1,0:T(1,128)}) custom-call(s32[256]{0:T(256)} %reshape.205.local_ref, s32[256]{0:T(256)} %fusion.58.query_ref, f32[32,128,128]{2,1,0:T(8,128)} %convert_add_fusion.pre_ref, bf16[64,32,128]{2,1,0:T(8,128)(2,1)} %bitcast.49), custom_call_target="tpu_custom_call" | custom-call | tf_op jit(solution)/shard_map/pallas_call | solution.py:184
  81.8 1.9 %slice_reduce_fusion = f32[256]{0:T(256)S(1)} fusion(f32[256,1,128]{2,1,0:T(1,128)} %get-tuple-element.9), kind=kLoop, calls=%fused_computation.35 | loop fusion | bytes 2048 | tf_op jit(solution)/shard_map/slice | solution.py:195
  84.0 12.7 %all_to_all.30 = f32[32,1,128]{2,1,0:T(1,128)S(1)} all-to-all(f32[32,1,128]{2,1,0:T(1,128)S(1)} %reshape.216), channel_id=1, replica_groups=mesh['dp'=8,'mp'=4] {'dp','mp'}, dimensions={0} | all-to-all | bytes 32768 | tf_op jit(solution)/shard_map/all_to_all | solution.py:125
  98.7 19.8 %shard_map.76 = (bf16[64,32,128]{2,1,0:T(8,128)(2,1)}, bf16[32,128,128]{2,1,0:T(8,128)(2,1)}) custom-call(s32[256]{0:T(256)} %reshape.205.local_ref, s32[256]{0:T(256)} %fusion.58.query_ref, f32[256]{0:T(256)} %subtract_select_fusion.grad_ref, f32[32,128,128]{2,1,0:T(8,128)} %convert_add_fusion.pre_ref, bf16[32,128,128]{2,1,0:T(8,128)(2,1)} %get-tuple-element.10.emb_ref, ...), custom_call_target="tpu_custom_call" | custom-call | tf_op jit(solution)/shard_map/pallas_call | solution.py:208
  118.6 2.7 %all-to-all-start.3 = ((bf16[32,2,32,128]{3,2,1,0:T(8,128)(2,1)}), bf16[32,2,32,128]{3,2,1,0:T(8,128)(2,1)S(1)}, u32[]{:S(2)}, u32[]{:S(2)}) async-start(bf16[32,2,32,128]{3,2,1,0:T(8,128)(2,1)} %bitcast.51), calls=%async_computation.3 | async-start | bytes 1048576 | tf_op jit(solution)/shard_map/all_to_all | solution.py:125
  121.3 1.7 collective-permute-start.9
  123.0 13.9 %all-to-all-done.3 = bf16[32,2,32,128]{3,2,1,0:T(8,128)(2,1)S(1)} async-done(((bf16[32,2,32,128]{3,2,1,0:T(8,128)(2,1)}), bf16[32,2,32,128]{3,2,1,0:T(8,128)(2,1)S(1)}, u32[]{:S(2)}, u32[]{:S(2)}) %all-to-all-start.3) | async-done | bytes 524320 | tf_op jit(solution)/shard_map/all_to_all | solution.py:125
  137.2 1.3 collective-permute-start.6
  138.5 13.8 %collective-permute-done.9 = bf16[32,128,128]{2,1,0:T(8,128)(2,1)S(1)} collective-permute-done((bf16[32,128,128]{2,1,0:T(8,128)(2,1)}, bf16[32,128,128]{2,1,0:T(8,128)(2,1)S(1)}, u32[]{:S(2)}, u32[]{:S(2)}) %collective-permute-start.9) | collective-permute-done | bytes 1048608 | tf_op jit(solution)/shard_map/ppermute | solution.py:90
  153.4 1.6 collective-permute-done.7
  155.3 1.4 broadcast_select_fusion.3
  157.3 2.3 %slice-done = s8[4194304]{0:T(1024)(128)(4,1)S(1)} async-done(((s8[6291456]{0:T(1024)(128)(4,1)}), s8[4194304]{0:T(1024)(128)(4,1)S(1)}, s32[]{:S(2)}) %slice-start) | async-done | bytes 4194328
  160.3 2.4 %fusion.19 = f32[128,192]{0,1:T(8,128)} fusion(f32[128,192]{0,1:T(8,128)S(1)} %convolution_bitcast_fusion.1, bf16[128,192,128]{2,1,0:T(8,128)(2,1)S(1)} %bitcast.48, bf16[64,128,128]{2,1,0:T(8,128)(2,1)S(1)} %get-tuple-element.21, bf16[64,128,128]{2,1,0:T(8,128)(2,1)S(1)} %get-tuple-element.20), kind=kOutput, calls=%fused_computation.22 | convolution fusion | flops 807428096 | bytes 10682368 | tf_op jit(solution)/shard_map/nhl,nle->he/dot_general | solution.py:231
  162.7 5.6 %all-to-all-start.4 = ((f32[8,24,128]{2,1,0:T(8,128)}), f32[8,24,128]{2,1,0:T(8,128)S(1)}, u32[]{:S(2)}, u32[]{:S(2)}) async-start(f32[8,24,128]{2,1,0:T(8,128)} %bitcast.10), calls=%async_computation.4 | async-start | bytes 196608 | tf_op jit(solution)/shard_map/all_to_all | solution.py:125
  169.3 6.2 %all-to-all-done.4 = f32[8,24,128]{2,1,0:T(8,128)S(1)} async-done(((f32[8,24,128]{2,1,0:T(8,128)}), f32[8,24,128]{2,1,0:T(8,128)S(1)}, u32[]{:S(2)}, u32[]{:S(2)}) %all-to-all-start.4) | async-done | bytes 98336 | tf_op jit(solution)/shard_map/all_to_all | solution.py:125
  176.2 3.4 %all-to-all-start.5 = ((f32[8,24,128]{2,1,0:T(8,128)}), f32[8,24,128]{2,1,0:T(8,128)S(1)}, u32[]{:S(2)}, u32[]{:S(2)}) async-start(f32[8,24,128]{2,1,0:T(8,128)} %broadcast_in_dim.104), calls=%async_computation.5 | async-start | bytes 196608 | tf_op jit(solution)/shard_map/all_to_all | solution.py:125
  179.5 8.2 %convolution_bitcast_fusion = f32[128,192,128]{2,1,0:T(8,128)} fusion(bf16[64,128,128]{2,1,0:T(8,128)(2,1)} %copy-done.1, bf16[64,128,128]{2,1,0:T(8,128)(2,1)S(1)} %get-tuple-element.20, bf16[192,128]{1,0:T(8,128)(2,1)S(1)} %copy-done.2), kind=kOutput, calls=%fused_computation.1 | convolution fusion | flops 807403520 | bytes 16826368 | tf_op jit(solution)/shard_map/nle,he->nhl/dot_general | solution.py:239
  (84 shorter events, 15.2 us)
Async XLA Ops:
  0.6 8.8 %copy-start = (bf16[8,32,192]{2,1,0:T(8,128)(2,1)S(1)}, bf16[8,32,192]{2,1,0:T(8,128)(2,1)}, u32[]{:S(2)}) copy-start(bf16[8,32,192]{2,1,0:T(8,128)(2,1)} %param.4) | copy-start | bytes 294916
  0.6 13.7 %copy-start.2 = (bf16[192,128]{1,0:T(8,128)(2,1)S(1)}, bf16[192,128]{1,0:T(8,128)(2,1)}, u32[]{:S(2)}) copy-start(bf16[192,128]{1,0:T(8,128)(2,1)} %param.6) | copy-start | bytes 147460
  2.1 18.1 %all-to-all-start = ((s32[32,1,128]{2,1,0:T(1,128)}), s32[32,1,128]{2,1,0:T(1,128)S(1)}, u32[]{:S(2)}, u32[]{:S(2)}) async-start(s32[32,1,128]{2,1,0:T(1,128)} %reshape.214), calls=%async_computation | async-start | bytes 32768 | tf_op jit(solution)/shard_map/all_to_all | solution.py:125
  10.3 11.5 %collective-permute-start.4 = (f32[2,32,128]{2,1,0:T(8,128)S(1)}, f32[2,32,128]{2,1,0:T(8,128)S(1)}, u32[]{:S(2)}, u32[]{:S(2)}) collective-permute-start(f32[2,32,128]{2,1,0:T(8,128)S(1)} %fusion.32), channel_id=1, source_target_pairs={{0,1},{1,0},{2,3},{3,2},{4,5},{5,4},{6,7},{7,6},{8,9},{9,8},{10,11... | collective-permute-start | bytes 98312 | tf_op jit(solution)/shard_map/ppermute | solution.py:90
  11.5 12.3 %collective-permute-start.3 = (f32[2,32,128]{2,1,0:T(8,128)S(1)}, f32[2,32,128]{2,1,0:T(8,128)S(1)}, u32[]{:S(2)}, u32[]{:S(2)}) collective-permute-start(f32[2,32,128]{2,1,0:T(8,128)S(1)} %fusion.35), channel_id=1, source_target_pairs={{0,1},{1,0},{2,3},{3,2},{4,5},{5,4},{6,7},{7,6},{8,9},{9,8},{10,11... | collective-permute-start | bytes 98312 | tf_op jit(solution)/shard_map/ppermute | solution.py:90
  14.0 12.2 %collective-permute-start.1 = (bf16[32,128,128]{2,1,0:T(8,128)(2,1)S(1)}, bf16[32,128,128]{2,1,0:T(8,128)(2,1)}, u32[]{:S(2)}, u32[]{:S(2)}) collective-permute-start(bf16[32,128,128]{2,1,0:T(8,128)(2,1)S(1)} %fusion.15), channel_id=1, source_target_pairs={{0,1},{1,0},{2,3},{3,2},{4,5},{5,4},{6,7},{7,6},{8,9},{9,8},{10,11... | collective-permute-start | bytes 3145736 | tf_op jit(solution)/shard_map/ppermute | solution.py:90
  17.5 22.8 %collective-permute-start = (bf16[32,128,128]{2,1,0:T(8,128)(2,1)}, bf16[32,128,128]{2,1,0:T(8,128)(2,1)}, u32[]{:S(2)}, u32[]{:S(2)}) collective-permute-start(bf16[32,128,128]{2,1,0:T(8,128)(2,1)} %fusion.10), channel_id=1, source_target_pairs={{0,1},{1,0},{2,3},{3,2},{4,5},{5,4},{6,7},{7,6},{8,9},{9,8},{10,11... | collective-permute-start | bytes 3145736 | tf_op jit(solution)/shard_map/ppermute | solution.py:90
  22.0 3.9 %collective-permute-start.5 = (f32[2,32,128]{2,1,0:T(8,128)S(1)}, f32[2,32,128]{2,1,0:T(8,128)S(1)}, u32[]{:S(2)}, u32[]{:S(2)}) collective-permute-start(f32[2,32,128]{2,1,0:T(8,128)S(1)} %convolution_add_fusion), channel_id=1, source_target_pairs={{0,2},{1,3},{2,0},{3,1},{4,6},{5,7},{6,4},{7,5},{8,10},{9,11},{10,... | collective-permute-start | bytes 98312 | tf_op jit(solution)/shard_map/ppermute | solution.py:90
  29.6 29.4 %collective-permute-start.2 = (bf16[32,128,128]{2,1,0:T(8,128)(2,1)}, bf16[32,128,128]{2,1,0:T(8,128)(2,1)}, u32[]{:S(2)}, u32[]{:S(2)}) collective-permute-start(bf16[32,128,128]{2,1,0:T(8,128)(2,1)} %add_convert_fusion), channel_id=1, source_target_pairs={{0,2},{1,3},{2,0},{3,1},{4,6},{5,7},{6,4},{7,5},{8,10},{9,11},{10,... | collective-permute-start | bytes 3145736 | tf_op jit(solution)/shard_map/ppermute | solution.py:90
  32.4 29.9 %all-to-all-start.1 = ((bf16[32,2,32,128]{3,2,1,0:T(8,128)(2,1)}), bf16[32,2,32,128]{3,2,1,0:T(8,128)(2,1)S(1)}, u32[]{:S(2)}, u32[]{:S(2)}) async-start(bf16[32,2,32,128]{3,2,1,0:T(8,128)(2,1)} %broadcast_in_dim.96), calls=%async_computation.1 | async-start | bytes 1048576 | tf_op jit(solution)/shard_map/all_to_all | solution.py:125
  62.3 21.4 %copy-start.5 = (s32[256]{0:T(256)S(1)}, s32[256]{0:T(256)}, u32[]{:S(2)}) copy-start(s32[256]{0:T(256)} %fusion.58.query_ref) | copy-start | bytes 3076
  62.3 0.8 copy-start.3
  118.6 36.7 %copy-start.4 = (bf16[32,128,128]{2,1,0:T(8,128)(2,1)S(1)}, bf16[32,128,128]{2,1,0:T(8,128)(2,1)}, u32[]{:S(2)}) copy-start(bf16[32,128,128]{2,1,0:T(8,128)(2,1)} %get-tuple-element.13) | copy-start | bytes 3145732
  118.6 18.3 %all-to-all-start.3 = ((bf16[32,2,32,128]{3,2,1,0:T(8,128)(2,1)}), bf16[32,2,32,128]{3,2,1,0:T(8,128)(2,1)S(1)}, u32[]{:S(2)}, u32[]{:S(2)}) async-start(bf16[32,2,32,128]{3,2,1,0:T(8,128)(2,1)} %bitcast.51), calls=%async_computation.3 | async-start | bytes 1048576 | tf_op jit(solution)/shard_map/all_to_all | solution.py:125
  121.3 31.0 %collective-permute-start.9 = (bf16[32,128,128]{2,1,0:T(8,128)(2,1)}, bf16[32,128,128]{2,1,0:T(8,128)(2,1)S(1)}, u32[]{:S(2)}, u32[]{:S(2)}) collective-permute-start(bf16[32,128,128]{2,1,0:T(8,128)(2,1)} %get-tuple-element.13), channel_id=1, source_target_pairs={{0,2},{1,3},{2,0},{3,1},{4,6},{5,7},{6,4},{7,5},{8,10},{9,11},{10,... | collective-permute-start | bytes 3145736 | tf_op jit(solution)/shard_map/ppermute | solution.py:90
  123.0 32.2 %collective-permute-start.11 = (bf16[32,128,128]{2,1,0:T(8,128)(2,1)}, bf16[32,128,128]{2,1,0:T(8,128)(2,1)}, u32[]{:S(2)}, u32[]{:S(2)}) collective-permute-start(bf16[32,128,128]{2,1,0:T(8,128)(2,1)} %get-tuple-element.13), channel_id=1, source_target_pairs={{0,1},{1,0},{2,3},{3,2},{4,5},{5,4},{6,7},{7,6},{8,9},{9,8},{10,11... | collective-permute-start | bytes 3145736 | tf_op jit(solution)/shard_map/ppermute | solution.py:90
  137.2 16.3 %collective-permute-start.8 = (bf16[2,32,128]{2,1,0:T(8,128)(2,1)S(1)}, bf16[2,32,128]{2,1,0:T(8,128)(2,1)S(1)}, u32[]{:S(2)}, u32[]{:S(2)}) collective-permute-start(bf16[2,32,128]{2,1,0:T(8,128)(2,1)S(1)} %fusion.24), channel_id=1, source_target_pairs={{0,1},{1,0},{2,3},{3,2},{4,5},{5,4},{6,7},{7,6},{8,9},{9,8},{10,11... | collective-permute-start | bytes 49160 | tf_op jit(solution)/shard_map/ppermute | solution.py:90
  137.2 15.7 %collective-permute-start.6 = (bf16[2,32,128]{2,1,0:T(8,128)(2,1)S(1)}, bf16[2,32,128]{2,1,0:T(8,128)(2,1)S(1)}, u32[]{:S(2)}, u32[]{:S(2)}) collective-permute-start(bf16[2,32,128]{2,1,0:T(8,128)(2,1)S(1)} %fusion.24), channel_id=1, source_target_pairs={{0,2},{1,3},{2,0},{3,1},{4,6},{5,7},{6,4},{7,5},{8,10},{9,11},{10,... | collective-permute-start | bytes 49160 | tf_op jit(solution)/shard_map/ppermute | solution.py:90
  152.3 4.3 %collective-permute-start.10 = (bf16[32,128,128]{2,1,0:T(8,128)(2,1)S(1)}, bf16[32,128,128]{2,1,0:T(8,128)(2,1)S(1)}, u32[]{:S(2)}, u32[]{:S(2)}) collective-permute-start(bf16[32,128,128]{2,1,0:T(8,128)(2,1)S(1)} %collective-permute-done.9), channel_id=1, source_target_pairs={{0,1},{1,0},{2,3},{3,2},{4,5},{5,4},{6,7},{7,6},{8,9},{9,8},{10,11... | collective-permute-start | bytes 3145736 | tf_op jit(solution)/shard_map/ppermute | solution.py:90
  152.9 2.1 %collective-permute-start.7 = (bf16[2,32,128]{2,1,0:T(8,128)(2,1)S(1)}, bf16[2,32,128]{2,1,0:T(8,128)(2,1)S(1)}, u32[]{:S(2)}, u32[]{:S(2)}) collective-permute-start(bf16[2,32,128]{2,1,0:T(8,128)(2,1)S(1)} %collective-permute-done.6), channel_id=1, source_target_pairs={{0,1},{1,0},{2,3},{3,2},{4,5},{5,4},{6,7},{7,6},{8,9},{9,8},{10,11... | collective-permute-start | bytes 49160 | tf_op jit(solution)/shard_map/ppermute | solution.py:90
  156.6 2.9 %slice-start = ((s8[6291456]{0:T(1024)(128)(4,1)}), s8[4194304]{0:T(1024)(128)(4,1)S(1)}, s32[]{:S(2)}) async-start(s8[6291456]{0:T(1024)(128)(4,1)} %bitcast.47), calls=%async_computation.6 | async-start | bytes 8388608
  156.8 3.5 %slice-start.1 = ((s8[6291456]{0:T(1024)(128)(4,1)}), s8[2097152]{0:T(1024)(128)(4,1)S(1)}, s32[]{:S(2)}) async-start(s8[6291456]{0:T(1024)(128)(4,1)} %bitcast.47), calls=%async_computation.7 | async-start | bytes 4194304
  157.3 5.5 %copy-start.1 = (bf16[64,128,128]{2,1,0:T(8,128)(2,1)}, bf16[64,128,128]{2,1,0:T(8,128)(2,1)S(1)}, u32[]{:S(2)}) copy-start(bf16[64,128,128]{2,1,0:T(8,128)(2,1)S(1)} %get-tuple-element.21) | copy-start | bytes 6291460
  162.7 12.7 %all-to-all-start.4 = ((f32[8,24,128]{2,1,0:T(8,128)}), f32[8,24,128]{2,1,0:T(8,128)S(1)}, u32[]{:S(2)}, u32[]{:S(2)}) async-start(f32[8,24,128]{2,1,0:T(8,128)} %bitcast.10), calls=%async_computation.4 | async-start | bytes 196608 | tf_op jit(solution)/shard_map/all_to_all | solution.py:125
  176.2 11.5 %all-to-all-start.5 = ((f32[8,24,128]{2,1,0:T(8,128)}), f32[8,24,128]{2,1,0:T(8,128)S(1)}, u32[]{:S(2)}, u32[]{:S(2)}) async-start(f32[8,24,128]{2,1,0:T(8,128)} %broadcast_in_dim.104), calls=%async_computation.5 | async-start | bytes 196608 | tf_op jit(solution)/shard_map/all_to_all | solution.py:125

commit v2 on v1

--- a/solution.py
+++ b/solution.py
@@ -30,53 +30,53 @@
     lax.fori_loop(0, pre_ref.shape[0], embed, 0)
 
     def slots(b, carry):
-        for u in range(BATCH):
-            s = b * BATCH + u
-            sim = lax.dot_general(
-                visitors_ref[query_ref[s]],
-                emb_ref[local_ref[s]],
+        first = b * BATCH
+        sims = [
+            lax.dot_general(
+                visitors_ref[query_ref[first + u]],
+                emb_ref[local_ref[first + u]],
                 (((1,), (1,)), ((), ())),
                 preferred_element_type=jnp.float32,
             )
-            expo = jnp.exp(sharpness * sim)
-            total = jnp.sum(expo, axis=-1, keepdims=True)
-            weights_ref[s] = expo / total
-            score = jnp.sum(jnp.log(total), axis=0, keepdims=True) / sharpness
-            scores_ref[s] = jnp.broadcast_to(score, scores_ref.shape[1:])
+            for u in range(BATCH)
+        ]
+        expos = [jnp.exp(sharpness * sim) for sim in sims]
+        totals = [jnp.sum(expo, axis=-1, keepdims=True) for expo in expos]
+        for u in range(BATCH):
+            weights_ref[first + u] = expos[u] / totals[u]
+        for u in range(BATCH):
+            score = jnp.sum(jnp.log(totals[u]), axis=0, keepdims=True) / sharpness
+            scores_ref[first + u] = jnp.broadcast_to(score, scores_ref.shape[1:])
         return carry
 
     lax.fori_loop(0, weights_ref.shape[0] // BATCH, slots, 0)
 
 
-def grad_kernel(
-    local_ref, query_ref, grad_ref, pre_ref, emb_ref, visitors_ref, weights_ref,
-    query_grad_ref, pre_grad_ref, query_sum, passage_sum
+def slot_grad_of(grad_ref, weights_ref, s):
+    return (grad_ref[s] * weights_ref[s]).astype(jnp.bfloat16)
+
+
+def passage_kernel(
+    local_ref, query_ref, grad_ref, pre_ref, visitors_ref, weights_ref, pre_grad_ref, passage_sum
 ):
-    query_sum[...] = jnp.zeros_like(query_sum)
     passage_sum[...] = jnp.zeros_like(passage_sum)
 
     def slots(b, carry):
-        found = []
-        for u in range(BATCH):
-            s = b * BATCH + u
-            p = local_ref[s]
-            q = query_ref[s]
-            sim_grad = (grad_ref[s] * weights_ref[s]).astype(jnp.bfloat16)
-            query_term = jnp.dot(sim_grad, emb_ref[p], preferred_element_type=jnp.float32)
-            passage_term = lax.dot_general(
-                sim_grad,
-                visitors_ref[q],
+        first = b * BATCH
+        terms = [
+            lax.dot_general(
+                slot_grad_of(grad_ref, weights_ref, first + u),
+                visitors_ref[query_ref[first + u]],
                 (((0,), (0,)), ((), ())),
                 preferred_element_type=jnp.float32,
             )
-            found.append((p, q, query_term, passage_term))
-        for p, q, query_term, passage_term in found:
-            query_sum[q] += query_term
-            passage_sum[p] += passage_term
+            for u in range(BATCH)
+        ]
+        for u in range(BATCH):
+            passage_sum[local_ref[first + u]] += terms[u]
         return carry
 
     lax.fori_loop(0, weights_ref.shape[0] // BATCH, slots, 0)
-    query_grad_ref[...] = query_sum[...].astype(jnp.bfloat16)
 
     def back(p, carry):
         unit, norm = unit_rows(pre_ref[p])
@@ -86,11 +86,34 @@
     lax.fori_loop(0, pre_ref.shape[0], back, 0)
 
 
+def query_kernel(
+    local_ref, query_ref, grad_ref, emb_ref, weights_ref, query_grad_ref, query_sum
+):
+    query_sum[...] = jnp.zeros_like(query_sum)
+
+    def slots(b, carry):
+        first = b * BATCH
+        terms = [
+            jnp.dot(
+                slot_grad_of(grad_ref, weights_ref, first + u),
+                emb_ref[local_ref[first + u]],
+                preferred_element_type=jnp.float32,
+            )
+            for u in range(BATCH)
+        ]
+        for u in range(BATCH):
+            query_sum[query_ref[first + u]] += terms[u]
+        return carry
+
+    lax.fori_loop(0, weights_ref.shape[0] // BATCH, slots, 0)
+    query_grad_ref[...] = query_sum[...].astype(jnp.bfloat16)
+
+
 def swap(array, bit, groups):
     return lax.ppermute(array, "mp", [(i, i ^ bit) for i in range(groups)])
 
 
-def reduce_mp(states, project, groups, dtype):
+def reduce_mp(states, project, groups, dtype, later=()):
     f32 = jnp.float32
     me = lax.axis_index("mp")
     rows = states.shape[0] // groups
@@ -99,12 +122,14 @@
         return project(lax.dynamic_slice_in_dim(states, index * rows, rows, 0))
 
     if groups != 4:
-        return lax.psum_scatter(project(states), "mp", scatter_dimension=0, tiled=True)
+        whole = lax.psum_scatter(project(states), "mp", scatter_dimension=0, tiled=True)
+        return whole, later
     far_out = swap(block(me ^ 3).astype(dtype), 1, groups)
     near_out = swap(block(me ^ 1).astype(dtype), 1, groups)
-    far = block(me ^ 2) + far_out.astype(f32)
-    far_in = swap(far.astype(dtype), 2, groups)
-    return (block(me) + near_out.astype(f32)) + far_in.astype(f32)
+    far = (block(me ^ 2) + far_out.astype(f32)).astype(dtype)
+    far, later = lax.optimization_barrier((far, later))
+    far_in = swap(far, 2, groups)
+    return (block(me) + near_out.astype(f32)) + far_in.astype(f32), later
 
 
 def gather_mp(mine, groups):
@@ -146,22 +171,23 @@
     slot_total = owners * capacity
     queries = owners * query_rows
 
-    listings = spread(candidates, both, owners).reshape(owners, requests)
-    query_pre = reduce_mp(
-        query_states,
-        lambda s: jnp.einsum("nlh,he->nle", s, projection, preferred_element_type=f32),
-        groups,
-        f32,
-    )
-    query_unit, query_norm = unit_rows(query_pre)
-    visitors = spread(query_unit.astype(jnp.bfloat16), both, owners)
-    visitors = visitors.reshape(queries, qry_len, emb_dim)
-    passage_pre = reduce_mp(
+    passage_pre, (query_late, candidates_late) = reduce_mp(
         passage_states,
         lambda s: jnp.einsum("nhl,he->nle", s, projection, preferred_element_type=f32),
         groups,
         jnp.bfloat16,
-    )
+        (query_states, candidates),
+    )
+    query_pre, _ = reduce_mp(
+        query_late,
+        lambda s: jnp.einsum("nlh,he->nle", s, projection, preferred_element_type=f32),
+        groups,
+        f32,
+    )
+    listings = spread(candidates_late, both, owners).reshape(owners, requests)
+    query_unit, query_norm = unit_rows(query_pre)
+    visitors = spread(query_unit.astype(jnp.bfloat16), both, owners)
+    visitors = visitors.reshape(queries, qry_len, emb_dim)
 
     held = (listings // passage_rows) == me
     within = jnp.cumsum(held.astype(jnp.int32), axis=1) - 1
@@ -205,20 +231,27 @@
     )
     losses = lax.dynamic_slice_in_dim(jnp.log(sums[0]) - sums[1], me * query_rows, query_rows)
 
-    query_terms, passage_pre_grad = pl.pallas_call(
-        grad_kernel,
-        out_shape=(
-            jax.ShapeDtypeStruct((queries, qry_len, emb_dim), jnp.bfloat16),
-            jax.ShapeDtypeStruct(block_shape, jnp.bfloat16),
+    passage_pre_grad = pl.pallas_call(
+        passage_kernel,
+        out_shape=jax.ShapeDtypeStruct(block_shape, jnp.bfloat16),
+        in_specs=[smem, smem, smem, vmem, vmem, vmem],
+        out_specs=vmem,
+        scratch_shapes=[pltpu.VMEM(block_shape, f32)],
+        compiler_params=params,
+    )(local_of, query_of, slot_grad, passage_pre, visitors, weights)
+    passage_pre_grad, slot_grad = lax.optimization_barrier((passage_pre_grad, slot_grad))
+    work = slot_total * qry_len * psg_len
+    query_terms = pl.pallas_call(
+        query_kernel,
+        out_shape=jax.ShapeDtypeStruct((queries, qry_len, emb_dim), jnp.bfloat16),
+        in_specs=[smem, smem, smem, vmem, vmem],
+        out_specs=vmem,
+        scratch_shapes=[pltpu.VMEM((queries, qry_len, emb_dim), f32)],
+        compiler_params=params,
+        cost_estimate=pl.CostEstimate(
+            flops=2 * work * emb_dim, bytes_accessed=4 * work, transcendentals=0
         ),
-        in_specs=[smem, smem, smem, vmem, vmem, vmem, vmem],
-        out_specs=(vmem, vmem),
-        scratch_shapes=[
-            pltpu.VMEM((queries, qry_len, emb_dim), f32),
-            pltpu.VMEM(block_shape, f32),
-        ],
-        compiler_params=params,
-    )(local_of, query_of, slot_grad, passage_pre, passage_emb, visitors, weights)
+    )(local_of, query_of, slot_grad, passage_emb, weights)
 
     terms_back = exchange(query_terms.reshape(owners, query_rows, qry_len, emb_dim), both)
     query_emb_grad = jnp.sum(
@@ -231,10 +264,8 @@
     weight_part = weight_part + jnp.einsum(
         "nhl,nle->he", passage_states, passage_all, preferred_element_type=f32
     )
-    height = weight_part.shape[0] // replicas
-    pieces = exchange(weight_part.reshape(replicas, height, emb_dim), "dp")
-    piece = jnp.sum(pieces.reshape(replicas, height, emb_dim), axis=0)
-    weight_grad = spread(piece, "dp", replicas).reshape(weight_part.shape)
+    shares = spread(weight_part.astype(jnp.bfloat16), "dp", replicas)
+    weight_grad = jnp.sum(shares.reshape((replicas,) + weight_part.shape).astype(f32), axis=0)
     query_grads = jnp.einsum("nle,he->nlh", query_all, projection, preferred_element_type=f32)
     passage_grads = jnp.einsum("nle,he->nhl", passage_all, projection, preferred_element_type=f32)
     return (losses, weight_grad, query_grads, passage_grads)

time: 189 us -> 195 us (1.032)
  Pallas kernels: 38.5 us -> 47.6 us
  waiting for transfers between devices: 56.4 us -> 62 us
  starting transfers between devices: 31.9 us -> 28.1 us
  blocking collectives: 12.7 us -> 10 us
  matrix products: 24.9 us -> 22.7 us
    all_to_all x5 -> x4, waiting for transfers between devices: 20.1 us -> 30.3 us  [exchange(): return lax.all_to_all(array, axes, split_axis=0, concat_axis=0, tiled=True)]
    pallas_call x1 -> x2, Pallas kernels: 19.8 us -> 28.9 us  [the longest x1 19.1 us: on_device(): pl.pallas_call(passage_kernel, out_shape=jax.ShapeDtypeStruct(block_shape...]
    ppermute x12, waiting for transfers between devices: 36.3 us -> 31.7 us  [swap(): return lax.ppermute(array, 'mp', [(i, i ^ bit) for i in range(groups)])]
    all_to_all x1, blocking collectives: 12.7 us -> 10 us  [exchange(): return lax.all_to_all(array, axes, split_axis=0, concat_axis=0, tiled=True)]
    all_to_all x5 -> x4, starting transfers between devices: 23.6 us -> 21.1 us  [exchange(): return lax.all_to_all(array, axes, split_axis=0, concat_axis=0, tiled=True)]
    unnamed x21 -> x22, local copies, waits for them, and re-layouts: 5.5 us -> 4.84 us
  transfers between devices with their start and end apart: 17 -> 16, of which waited for: 6 -> 7; matrix products, arithmetic and copies ran while one was open for 18% -> 16% of each run, Pallas kernels for 0% -> 0%
where the time goes in v2:
time: 195 us; the launch traced here: 194 us
  waiting for transfers between devices  62 us (32%)
  Pallas kernels  47.6 us (24%)
  starting transfers between devices  28.1 us (14%)
  matrix products  22.7 us (12%)
  other arithmetic  11.3 us (6%)
  local copies, waits for them, and re-layouts  11.2 us (6%)
  blocking collectives  10 us (5%)
    ppermute x12, waiting for transfers between devices, swap(): return lax.ppermute(array, 'mp', [(i, i ^ bit) for i in range(groups)])  31.7 us
    all_to_all x4, waiting for transfers between devices, exchange(): return lax.all_to_all(array, axes, split_axis=0, concat_axis=0, tiled=True)  30.3 us
    all_to_all x4, starting transfers between devices, exchange(): return lax.all_to_all(array, axes, split_axis=0, concat_axis=0, tiled=True)  21.1 us
    pallas_call x1, Pallas kernels, on_device(): pl.pallas_call(passage_kernel, out_shape=jax.ShapeDtypeStruct(block_shape...  19.1 us
    pallas_call x1, Pallas kernels, on_device(): pl.pallas_call(score_kernel, out_shape=(jax.ShapeDtypeStruct(block_shape,...  18.7 us
    dot_general x4, matrix products, on_device(): jnp.einsum('nhl,he->nle', s, projection, preferred_element_type=f32)  11 us
    all_to_all x1, blocking collectives, exchange(): return lax.all_to_all(array, axes, split_axis=0, concat_axis=0, tiled=True)  10 us
    pallas_call x1, Pallas kernels, on_device(): pl.pallas_call(query_kernel, out_shape=jax.ShapeDtypeStruct((queries, qry...  9.76 us
  transfers between devices with their start and end apart: 16, of which 7 were waited for; matrix products, arithmetic and copies ran while one was open for 16% of the time, Pallas kernels for 0%

profile of v2, /device:TPU:0, one launch (start us, length us, event | category | flops | bytes accessed | tf_op | source)
XLA Modules:
  0.0 193.9 jit_solution(12184978370481488607)
XLA Ops:
  0.7 2.2 %fusion.12 = bf16[32,128,128]{2,1,0:T(8,128)(2,1)S(1)} fusion(bf16[128,192,128]{2,1,0:T(8,128)(2,1)} %param.5, s32[]{:T(128)S(6)} %select_n.163, bf16[192,128]{1,0:T(8,128)(2,1)} %param.6), kind=kOutput, calls=%fused_computation.18 | convolution fusion | flops 201850880 | bytes 2670596 | tf_op jit(solution)/shard_map/nhl,he->nle/dot_general | solution.py:176
  3.4 3.2 %fusion.15 = bf16[32,128,128]{2,1,0:T(8,128)(2,1)} fusion(bf16[128,192,128]{2,1,0:T(8,128)(2,1)} %param.5, s32[]{:T(128)S(6)} %select_n.170, bf16[192,128]{1,0:T(8,128)(2,1)S(1)} %copy-done.2), kind=kOutput, calls=%fused_computation.19 | convolution fusion | flops 201850880 | bytes 2670596 | tf_op jit(solution)/shard_map/nhl,he->nle/dot_general | solution.py:176
  6.8 2.2 %fusion.4 = f32[32,128,128]{2,1,0:T(8,128)S(1)} fusion(bf16[128,192,128]{2,1,0:T(8,128)(2,1)} %param.5, s32[]{:T(128)S(6)} %select_n.169, bf16[192,128]{1,0:T(8,128)(2,1)S(1)} %copy-done.2), kind=kOutput, calls=%fused_computation.12 | convolution fusion | flops 201326592 | bytes 3719172 | tf_op jit(solution)/shard_map/nhl,he->nle/dot_general | solution.py:176
  9.0 3.5 %add_convert_fusion = bf16[32,128,128]{2,1,0:T(8,128)(2,1)} fusion(bf16[32,128,128]{2,1,0:T(8,128)(2,1)} %collective-permute-done, bf16[128,192,128]{2,1,0:T(8,128)(2,1)} %param.5, s32[]{:T(128)S(6)} %select_n.162, bf16[192,128]{1,0:T(8,128)(2,1)S(1)} %copy-done.2), kind=kOutput, calls=%fused_computation.7 | convolution fusion | flops 202899456 | bytes 3719172 | tf_op jit(solution)/shard_map/nhl,he->nle/dot_general | solution.py:176
  13.2 7.3 %all-to-all-start = ((s32[32,1,128]{2,1,0:T(1,128)}), s32[32,1,128]{2,1,0:T(1,128)S(1)}, u32[]{:S(2)}, u32[]{:S(2)}) async-start(s32[32,1,128]{2,1,0:T(1,128)} %reshape.206), calls=%async_computation | async-start | bytes 32768 | tf_op jit(solution)/shard_map/all_to_all | solution.py:150
  21.3 1.8 collective-permute-start.2
  23.1 4.5 %all-to-all-done = s32[32,1,128]{2,1,0:T(1,128)S(1)} async-done(((s32[32,1,128]{2,1,0:T(1,128)}), s32[32,1,128]{2,1,0:T(1,128)S(1)}, u32[]{:S(2)}, u32[]{:S(2)}) %all-to-all-start) | async-done | bytes 16416 | tf_op jit(solution)/shard_map/all_to_all | solution.py:150
  30.0 17.7 %collective-permute-done.5 = f32[2,32,128]{2,1,0:T(8,128)S(1)} collective-permute-done((f32[2,32,128]{2,1,0:T(8,128)S(1)}, f32[2,32,128]{2,1,0:T(8,128)S(1)}, u32[]{:S(2)}, u32[]{:S(2)}) %collective-permute-start.5) | collective-permute-done | bytes 32800 | tf_op jit(solution)/shard_map/ppermute | solution.py:113
  48.0 0.9 broadcast_in_dim.96
  48.9 5.6 %all-to-all-start.1 = ((bf16[32,2,32,128]{3,2,1,0:T(8,128)(2,1)}), bf16[32,2,32,128]{3,2,1,0:T(8,128)(2,1)S(1)}, u32[]{:S(2)}, u32[]{:S(2)}) async-start(bf16[32,2,32,128]{3,2,1,0:T(8,128)(2,1)} %broadcast_in_dim.96), calls=%async_computation.1 | async-start | bytes 1048576 | tf_op jit(solution)/shard_map/all_to_all | solution.py:150
  55.3 1.2 select_reduce_fusion.1
  57.8 3.3 %convert_add_fusion.pre_ref = f32[32,128,128]{2,1,0:T(8,128)} fusion(bf16[32,128,128]{2,1,0:T(8,128)(2,1)} %collective-permute-done.2, f32[32,128,128]{2,1,0:T(8,128)S(1)} %fusion.4, bf16[32,128,128]{2,1,0:T(8,128)(2,1)} %collective-permute-done.1), kind=kLoop, calls=%fused_computation.6 | loop fusion | flops 2097152 | bytes 6291456 | tf_op jit(solution)/shard_map/add | solution.py:132
  61.1 9.0 %all-to-all-done.1 = bf16[32,2,32,128]{3,2,1,0:T(8,128)(2,1)S(1)} async-done(((bf16[32,2,32,128]{3,2,1,0:T(8,128)(2,1)}), bf16[32,2,32,128]{3,2,1,0:T(8,128)(2,1)S(1)}, u32[]{:S(2)}, u32[]{:S(2)}) %all-to-all-start.1) | async-done | bytes 524320 | tf_op jit(solution)/shard_map/all_to_all | solution.py:150
  70.1 0.8 copy-done.3
  70.9 18.7 %shard_map.75 = (bf16[32,128,128]{2,1,0:T(8,128)(2,1)}, f32[256,32,128]{2,1,0:T(8,128)}, f32[256,1,128]{2,1,0:T(1,128)}) custom-call(s32[256]{0:T(256)} %reshape.199.local_ref, s32[256]{0:T(256)} %fusion.60.query_ref, f32[32,128,128]{2,1,0:T(8,128)} %convert_add_fusion.pre_ref, bf16[64,32,128]{2,1,0:T(8,128)(2,1)} %bitcast.51), custom_call_target="tpu_custom_call" | custom-call | tf_op jit(solution)/shard_map/pallas_call | solution.py:210
  89.6 1.9 slice_reduce_fusion
  91.8 10.0 %all_to_all.25 = f32[32,1,128]{2,1,0:T(1,128)S(1)} all-to-all(f32[32,1,128]{2,1,0:T(1,128)S(1)} %reshape.208), channel_id=1, replica_groups=mesh['dp'=8,'mp'=4] {'dp','mp'}, dimensions={0} | all-to-all | bytes 32768 | tf_op jit(solution)/shard_map/all_to_all | solution.py:150
  103.8 19.1 %shard_map.76 = bf16[32,128,128]{2,1,0:T(8,128)(2,1)} custom-call(s32[256]{0:T(256)} %reshape.199.local_ref, s32[256]{0:T(256)} %fusion.60.query_ref, f32[256]{0:T(256)} %subtract_select_fusion.grad_ref, f32[32,128,128]{2,1,0:T(8,128)} %convert_add_fusion.pre_ref, bf16[64,32,128]{2,1,0:T(8,128)(2,1)} %bitcast.52, f32[256,32,128]{2,1,0:T(8,128)} %get-tuple-element.16.weights_ref), custom_call_target="tpu_custom_call" | custom-call | tf_op jit(solution)/shard_map/pallas_call | solution.py:234
  123.0 9.8 %shard_map.77 = bf16[64,32,128]{2,1,0:T(8,128)(2,1)} custom-call(s32[256]{0:T(256)} %reshape.199.local_ref, s32[256]{0:T(256)} %fusion.60.query_ref, f32[256]{0:T(256)} %subtract_select_fusion.grad_ref, bf16[32,128,128]{2,1,0:T(8,128)(2,1)} %get-tuple-element.18.emb_ref, f32[256,32,128]{2,1,0:T(8,128)} %get-tuple-element.16.weights_ref), custom_call_target="tpu_custom_call" | custom-call | flops 268435456 | bytes 4194304 | tf_op jit(solution)/shard_map/pallas_call | solution.py:244
  132.7 2.6 %all-to-all-start.3 = ((bf16[32,2,32,128]{3,2,1,0:T(8,128)(2,1)}), bf16[32,2,32,128]{3,2,1,0:T(8,128)(2,1)S(1)}, u32[]{:S(2)}, u32[]{:S(2)}) async-start(bf16[32,2,32,128]{3,2,1,0:T(8,128)(2,1)} %bitcast.53), calls=%async_computation.3 | async-start | bytes 1048576 | tf_op jit(solution)/shard_map/all_to_all | solution.py:150
  135.3 1.7 collective-permute-start.9
  137.0 13.9 %all-to-all-done.3 = bf16[32,2,32,128]{3,2,1,0:T(8,128)(2,1)S(1)} async-done(((bf16[32,2,32,128]{3,2,1,0:T(8,128)(2,1)}), bf16[32,2,32,128]{3,2,1,0:T(8,128)(2,1)S(1)}, u32[]{:S(2)}, u32[]{:S(2)}) %all-to-all-start.3) | async-done | bytes 524320 | tf_op jit(solution)/shard_map/all_to_all | solution.py:150
  151.2 1.3 collective-permute-start.6
  152.5 13.8 %collective-permute-done.9 = bf16[32,128,128]{2,1,0:T(8,128)(2,1)S(1)} collective-permute-done((bf16[32,128,128]{2,1,0:T(8,128)(2,1)S(1)}, bf16[32,128,128]{2,1,0:T(8,128)(2,1)S(1)}, u32[]{:S(2)}, u32[]{:S(2)}) %collective-permute-start.9) | collective-permute-done | bytes 1048608 | tf_op jit(solution)/shard_map/ppermute | solution.py:113
  167.5 1.4 broadcast_select_fusion.3
  169.9 2.3 %slice-done = s8[4194304]{0:T(1024)(128)(4,1)S(1)} async-done(((s8[6291456]{0:T(1024)(128)(4,1)}), s8[4194304]{0:T(1024)(128)(4,1)S(1)}, s32[]{:S(2)}) %slice-start) | async-done | bytes 4194328
  172.9 1.8 fusion.21
  174.7 0.8 broadcast_in_dim.104
  175.6 5.6 %all-to-all-start.4 = ((bf16[8,192,128]{2,1,0:T(8,128)(2,1)}), bf16[8,192,128]{2,1,0:T(8,128)(2,1)S(1)}, u32[]{:S(2)}, u32[]{:S(2)}) async-start(bf16[8,192,128]{2,1,0:T(8,128)(2,1)} %broadcast_in_dim.104), calls=%async_computation.4 | async-start | bytes 786432 | tf_op jit(solution)/shard_map/all_to_all | solution.py:150
  181.2 0.9 fusion.32
  182.1 8.2 %convolution_bitcast_fusion = f32[128,192,128]{2,1,0:T(8,128)} fusion(bf16[64,128,128]{2,1,0:T(8,128)(2,1)} %copy-done.1, bf16[64,128,128]{2,1,0:T(8,128)(2,1)S(1)} %get-tuple-element.26, bf16[192,128]{1,0:T(8,128)(2,1)S(1)} %copy-done.2), kind=kOutput, calls=%fused_computation.1 | convolution fusion | flops 807403520 | bytes 16826368 | tf_op jit(solution)/shard_map/nle,he->nhl/dot_general | solution.py:270
  190.3 2.9 %all-to-all-done.4 = bf16[8,192,128]{2,1,0:T(8,128)(2,1)S(1)} async-done(((bf16[8,192,128]{2,1,0:T(8,128)(2,1)}), bf16[8,192,128]{2,1,0:T(8,128)(2,1)S(1)}, u32[]{:S(2)}, u32[]{:S(2)}) %all-to-all-start.4) | async-done | bytes 393248 | tf_op jit(solution)/shard_map/all_to_all | solution.py:150
  (84 shorter events, 13.2 us)
Async XLA Ops:
  0.6 19.9 %copy-start = (bf16[8,32,192]{2,1,0:T(8,128)(2,1)S(1)}, bf16[8,32,192]{2,1,0:T(8,128)(2,1)}, u32[]{:S(2)}) copy-start(bf16[8,32,192]{2,1,0:T(8,128)(2,1)} %param.4) | copy-start | bytes 294916
  0.6 2.8 %copy-start.2 = (bf16[192,128]{1,0:T(8,128)(2,1)S(1)}, bf16[192,128]{1,0:T(8,128)(2,1)}, u32[]{:S(2)}) copy-start(bf16[192,128]{1,0:T(8,128)(2,1)} %param.6) | copy-start | bytes 147460
  2.9 6.1 %collective-permute-start = (bf16[32,128,128]{2,1,0:T(8,128)(2,1)S(1)}, bf16[32,128,128]{2,1,0:T(8,128)(2,1)}, u32[]{:S(2)}, u32[]{:S(2)}) collective-permute-start(bf16[32,128,128]{2,1,0:T(8,128)(2,1)S(1)} %fusion.12), channel_id=1, source_target_pairs={{0,1},{1,0},{2,3},{3,2},{4,5},{5,4},{6,7},{7,6},{8,9},{9,8},{10,11... | collective-permute-start | bytes 3145736 | tf_op jit(solution)/shard_map/ppermute | solution.py:113
  6.6 51.2 %collective-permute-start.1 = (bf16[32,128,128]{2,1,0:T(8,128)(2,1)}, bf16[32,128,128]{2,1,0:T(8,128)(2,1)}, u32[]{:S(2)}, u32[]{:S(2)}) collective-permute-start(bf16[32,128,128]{2,1,0:T(8,128)(2,1)} %fusion.15), channel_id=1, source_target_pairs={{0,1},{1,0},{2,3},{3,2},{4,5},{5,4},{6,7},{7,6},{8,9},{9,8},{10,11... | collective-permute-start | bytes 3145736 | tf_op jit(solution)/shard_map/ppermute | solution.py:113
  9.0 3.5 %copy-start.6 = (s32[2,64]{1,0:T(2,128)S(1)}, s32[2,64]{1,0:T(2,128)}, u32[]{:S(2)}) copy-start(s32[2,64]{1,0:T(2,128)} %param.7) | copy-start | bytes 1540
  13.2 14.4 %all-to-all-start = ((s32[32,1,128]{2,1,0:T(1,128)}), s32[32,1,128]{2,1,0:T(1,128)S(1)}, u32[]{:S(2)}, u32[]{:S(2)}) async-start(s32[32,1,128]{2,1,0:T(1,128)} %reshape.206), calls=%async_computation | async-start | bytes 32768 | tf_op jit(solution)/shard_map/all_to_all | solution.py:150
  20.8 9.2 %collective-permute-start.3 = (f32[2,32,128]{2,1,0:T(8,128)S(1)}, f32[2,32,128]{2,1,0:T(8,128)S(1)}, u32[]{:S(2)}, u32[]{:S(2)}) collective-permute-start(f32[2,32,128]{2,1,0:T(8,128)S(1)} %fusion.37), channel_id=1, source_target_pairs={{0,1},{1,0},{2,3},{3,2},{4,5},{5,4},{6,7},{7,6},{8,9},{9,8},{10,11... | collective-permute-start | bytes 98312 | tf_op jit(solution)/shard_map/ppermute | solution.py:113
  21.1 8.2 %collective-permute-start.4 = (f32[2,32,128]{2,1,0:T(8,128)S(1)}, f32[2,32,128]{2,1,0:T(8,128)S(1)}, u32[]{:S(2)}, u32[]{:S(2)}) collective-permute-start(f32[2,32,128]{2,1,0:T(8,128)S(1)} %fusion.34), channel_id=1, source_target_pairs={{0,1},{1,0},{2,3},{3,2},{4,5},{5,4},{6,7},{7,6},{8,9},{9,8},{10,11... | collective-permute-start | bytes 98312 | tf_op jit(solution)/shard_map/ppermute | solution.py:113
  21.3 36.5 %collective-permute-start.2 = (bf16[32,128,128]{2,1,0:T(8,128)(2,1)}, bf16[32,128,128]{2,1,0:T(8,128)(2,1)}, u32[]{:S(2)}, u32[]{:S(2)}) collective-permute-start(bf16[32,128,128]{2,1,0:T(8,128)(2,1)} %add_convert_fusion), channel_id=1, source_target_pairs={{0,2},{1,3},{2,0},{3,1},{4,6},{5,7},{6,4},{7,5},{8,10},{9,11},{10,... | collective-permute-start | bytes 3145736 | tf_op jit(solution)/shard_map/ppermute | solution.py:113
  29.4 18.2 %collective-permute-start.5 = (f32[2,32,128]{2,1,0:T(8,128)S(1)}, f32[2,32,128]{2,1,0:T(8,128)S(1)}, u32[]{:S(2)}, u32[]{:S(2)}) collective-permute-start(f32[2,32,128]{2,1,0:T(8,128)S(1)} %convolution_add_fusion), channel_id=1, source_target_pairs={{0,2},{1,3},{2,0},{3,1},{4,6},{5,7},{6,4},{7,5},{8,10},{9,11},{10,... | collective-permute-start | bytes 98312 | tf_op jit(solution)/shard_map/ppermute | solution.py:113
  48.9 21.2 %all-to-all-start.1 = ((bf16[32,2,32,128]{3,2,1,0:T(8,128)(2,1)}), bf16[32,2,32,128]{3,2,1,0:T(8,128)(2,1)S(1)}, u32[]{:S(2)}, u32[]{:S(2)}) async-start(bf16[32,2,32,128]{3,2,1,0:T(8,128)(2,1)} %broadcast_in_dim.96), calls=%async_computation.1 | async-start | bytes 1048576 | tf_op jit(solution)/shard_map/all_to_all | solution.py:150
  61.1 30.4 %copy-start.5 = (s32[256]{0:T(256)S(1)}, s32[256]{0:T(256)}, u32[]{:S(2)}) copy-start(s32[256]{0:T(256)} %fusion.60.query_ref) | copy-start | bytes 3076
  70.1 0.8 copy-start.3
  123.0 12.4 %copy-start.4 = (bf16[32,128,128]{2,1,0:T(8,128)(2,1)S(1)}, bf16[32,128,128]{2,1,0:T(8,128)(2,1)}, u32[]{:S(2)}) copy-start(bf16[32,128,128]{2,1,0:T(8,128)(2,1)} %shard_map.76) | copy-start | bytes 3145732
  132.7 18.2 %all-to-all-start.3 = ((bf16[32,2,32,128]{3,2,1,0:T(8,128)(2,1)}), bf16[32,2,32,128]{3,2,1,0:T(8,128)(2,1)S(1)}, u32[]{:S(2)}, u32[]{:S(2)}) async-start(bf16[32,2,32,128]{3,2,1,0:T(8,128)(2,1)} %bitcast.53), calls=%async_computation.3 | async-start | bytes 1048576 | tf_op jit(solution)/shard_map/all_to_all | solution.py:150
  135.3 31.0 %collective-permute-start.9 = (bf16[32,128,128]{2,1,0:T(8,128)(2,1)S(1)}, bf16[32,128,128]{2,1,0:T(8,128)(2,1)S(1)}, u32[]{:S(2)}, u32[]{:S(2)}) collective-permute-start(bf16[32,128,128]{2,1,0:T(8,128)(2,1)S(1)} %copy-done.4), channel_id=1, source_target_pairs={{0,2},{1,3},{2,0},{3,1},{4,6},{5,7},{6,4},{7,5},{8,10},{9,11},{10,... | collective-permute-start | bytes 3145736 | tf_op jit(solution)/shard_map/ppermute | solution.py:113
  137.0 30.4 %collective-permute-start.11 = (bf16[32,128,128]{2,1,0:T(8,128)(2,1)S(1)}, bf16[32,128,128]{2,1,0:T(8,128)(2,1)}, u32[]{:S(2)}, u32[]{:S(2)}) collective-permute-start(bf16[32,128,128]{2,1,0:T(8,128)(2,1)S(1)} %copy-done.4), channel_id=1, source_target_pairs={{0,1},{1,0},{2,3},{3,2},{4,5},{5,4},{6,7},{7,6},{8,9},{9,8},{10,11... | collective-permute-start | bytes 3145736 | tf_op jit(solution)/shard_map/ppermute | solution.py:113
  151.2 16.3 %collective-permute-start.8 = (bf16[2,32,128]{2,1,0:T(8,128)(2,1)S(1)}, bf16[2,32,128]{2,1,0:T(8,128)(2,1)S(1)}, u32[]{:S(2)}, u32[]{:S(2)}) collective-permute-start(bf16[2,32,128]{2,1,0:T(8,128)(2,1)S(1)} %fusion.26), channel_id=1, source_target_pairs={{0,1},{1,0},{2,3},{3,2},{4,5},{5,4},{6,7},{7,6},{8,9},{9,8},{10,11... | collective-permute-start | bytes 49160 | tf_op jit(solution)/shard_map/ppermute | solution.py:113
  151.2 15.7 %collective-permute-start.6 = (bf16[2,32,128]{2,1,0:T(8,128)(2,1)S(1)}, bf16[2,32,128]{2,1,0:T(8,128)(2,1)S(1)}, u32[]{:S(2)}, u32[]{:S(2)}) collective-permute-start(bf16[2,32,128]{2,1,0:T(8,128)(2,1)S(1)} %fusion.26), channel_id=1, source_target_pairs={{0,2},{1,3},{2,0},{3,1},{4,6},{5,7},{6,4},{7,5},{8,10},{9,11},{10,... | collective-permute-start | bytes 49160 | tf_op jit(solution)/shard_map/ppermute | solution.py:113
  166.3 2.9 %collective-permute-start.10 = (bf16[32,128,128]{2,1,0:T(8,128)(2,1)S(1)}, bf16[32,128,128]{2,1,0:T(8,128)(2,1)S(1)}, u32[]{:S(2)}, u32[]{:S(2)}) collective-permute-start(bf16[32,128,128]{2,1,0:T(8,128)(2,1)S(1)} %collective-permute-done.9), channel_id=1, source_target_pairs={{0,1},{1,0},{2,3},{3,2},{4,5},{5,4},{6,7},{7,6},{8,9},{9,8},{10,11... | collective-permute-start | bytes 3145736 | tf_op jit(solution)/shard_map/ppermute | solution.py:113
  166.9 2.1 %collective-permute-start.7 = (bf16[2,32,128]{2,1,0:T(8,128)(2,1)S(1)}, bf16[2,32,128]{2,1,0:T(8,128)(2,1)S(1)}, u32[]{:S(2)}, u32[]{:S(2)}) collective-permute-start(bf16[2,32,128]{2,1,0:T(8,128)(2,1)S(1)} %collective-permute-done.6), channel_id=1, source_target_pairs={{0,1},{1,0},{2,3},{3,2},{4,5},{5,4},{6,7},{7,6},{8,9},{9,8},{10,11... | collective-permute-start | bytes 49160 | tf_op jit(solution)/shard_map/ppermute | solution.py:113
  169.3 2.9 %slice-start = ((s8[6291456]{0:T(1024)(128)(4,1)}), s8[4194304]{0:T(1024)(128)(4,1)S(1)}, s32[]{:S(2)}) async-start(s8[6291456]{0:T(1024)(128)(4,1)} %bitcast.49), calls=%async_computation.5 | async-start | bytes 8388608
  169.4 3.5 %slice-start.1 = ((s8[6291456]{0:T(1024)(128)(4,1)}), s8[2097152]{0:T(1024)(128)(4,1)S(1)}, s32[]{:S(2)}) async-start(s8[6291456]{0:T(1024)(128)(4,1)} %bitcast.49), calls=%async_computation.6 | async-start | bytes 4194304
  169.9 4.8 %copy-start.1 = (bf16[64,128,128]{2,1,0:T(8,128)(2,1)}, bf16[64,128,128]{2,1,0:T(8,128)(2,1)S(1)}, u32[]{:S(2)}) copy-start(bf16[64,128,128]{2,1,0:T(8,128)(2,1)S(1)} %get-tuple-element.27) | copy-start | bytes 6291460
  175.6 17.6 %all-to-all-start.4 = ((bf16[8,192,128]{2,1,0:T(8,128)(2,1)}), bf16[8,192,128]{2,1,0:T(8,128)(2,1)S(1)}, u32[]{:S(2)}, u32[]{:S(2)}) async-start(bf16[8,192,128]{2,1,0:T(8,128)(2,1)} %broadcast_in_dim.104), calls=%async_computation.4 | async-start | bytes 786432 | tf_op jit(solution)/shard_map/all_to_all | solution.py:150

commit v3 on v1

--- a/solution.py
+++ b/solution.py
@@ -90,7 +90,7 @@
     return lax.ppermute(array, "mp", [(i, i ^ bit) for i in range(groups)])
 
 
-def reduce_mp(states, project, groups, dtype):
+def reduce_mp(states, project, groups, dtype, later=()):
     f32 = jnp.float32
     me = lax.axis_index("mp")
     rows = states.shape[0] // groups
@@ -99,12 +99,15 @@
         return project(lax.dynamic_slice_in_dim(states, index * rows, rows, 0))
 
     if groups != 4:
-        return lax.psum_scatter(project(states), "mp", scatter_dimension=0, tiled=True)
+        whole = lax.psum_scatter(project(states), "mp", scatter_dimension=0, tiled=True)
+        return whole, later
     far_out = swap(block(me ^ 3).astype(dtype), 1, groups)
     near_out = swap(block(me ^ 1).astype(dtype), 1, groups)
-    far = block(me ^ 2) + far_out.astype(f32)
-    far_in = swap(far.astype(dtype), 2, groups)
-    return (block(me) + near_out.astype(f32)) + far_in.astype(f32)
+    far = (block(me ^ 2) + far_out.astype(f32)).astype(dtype)
+    if later:
+        far, later = lax.optimization_barrier((far, later))
+    far_in = swap(far, 2, groups)
+    return (block(me) + near_out.astype(f32)) + far_in.astype(f32), later
 
 
 def gather_mp(mine, groups):
@@ -146,8 +149,7 @@
     slot_total = owners * capacity
     queries = owners * query_rows
 
-    listings = spread(candidates, both, owners).reshape(owners, requests)
-    query_pre = reduce_mp(
+    query_pre, _ = reduce_mp(
         query_states,
         lambda s: jnp.einsum("nlh,he->nle", s, projection, preferred_element_type=f32),
         groups,
@@ -156,12 +158,14 @@
     query_unit, query_norm = unit_rows(query_pre)
     visitors = spread(query_unit.astype(jnp.bfloat16), both, owners)
     visitors = visitors.reshape(queries, qry_len, emb_dim)
-    passage_pre = reduce_mp(
+    passage_pre, (candidates_late,) = reduce_mp(
         passage_states,
         lambda s: jnp.einsum("nhl,he->nle", s, projection, preferred_element_type=f32),
         groups,
         jnp.bfloat16,
-    )
+        (candidates,),
+    )
+    listings = spread(candidates_late, both, owners).reshape(owners, requests)
 
     held = (listings // passage_rows) == me
     within = jnp.cumsum(held.astype(jnp.int32), axis=1) - 1
@@ -231,10 +235,8 @@
     weight_part = weight_part + jnp.einsum(
         "nhl,nle->he", passage_states, passage_all, preferred_element_type=f32
     )
-    height = weight_part.shape[0] // replicas
-    pieces = exchange(weight_part.reshape(replicas, height, emb_dim), "dp")
-    piece = jnp.sum(pieces.reshape(replicas, height, emb_dim), axis=0)
-    weight_grad = spread(piece, "dp", replicas).reshape(weight_part.shape)
+    shares = spread(weight_part.astype(jnp.bfloat16), "dp", replicas)
+    weight_grad = jnp.sum(shares.reshape((replicas,) + weight_part.shape).astype(f32), axis=0)
     query_grads = jnp.einsum("nle,he->nlh", query_all, projection, preferred_element_type=f32)
     passage_grads = jnp.einsum("nle,he->nhl", passage_all, projection, preferred_element_type=f32)
     return (losses, weight_grad, query_grads, passage_grads)

time: 189 us -> 182 us (0.963)
  starting transfers between devices: 31.9 us -> 26.8 us
  waiting for transfers between devices: 56.4 us -> 54.2 us
    all_to_all x5 -> x4, starting transfers between devices: 23.6 us -> 17.3 us  [exchange(): return lax.all_to_all(array, axes, split_axis=0, concat_axis=0, tiled=True)]
    ppermute x12, waiting for transfers between devices: 36.3 us -> 32.3 us  [swap(): return lax.ppermute(array, 'mp', [(i, i ^ bit) for i in range(groups)])]
    all_to_all x5 -> x4, waiting for transfers between devices: 20.1 us -> 21.9 us  [exchange(): return lax.all_to_all(array, axes, split_axis=0, concat_axis=0, tiled=True)]
    unnamed x21 -> x22, local copies, waits for them, and re-layouts: 5.5 us -> 5.73 us
  transfers between devices with their start and end apart: 17 -> 16, of which waited for: 6 -> 7; matrix products, arithmetic and copies ran while one was open for 18% -> 19% of each run, Pallas kernels for 0% -> 0%
where the time goes in v3:
time: 182 us; the launch traced here: 181 us
  waiting for transfers between devices  54.2 us (30%)
  Pallas kernels  38.5 us (21%)
  starting transfers between devices  26.8 us (15%)
  matrix products  24.3 us (13%)
  blocking collectives  12.6 us (7%)
  local copies, waits for them, and re-layouts  12.1 us (7%)
  other arithmetic  11.3 us (6%)
    ppermute x12, waiting for transfers between devices, swap(): return lax.ppermute(array, 'mp', [(i, i ^ bit) for i in range(groups)])  32.3 us
    all_to_all x4, waiting for transfers between devices, exchange(): return lax.all_to_all(array, axes, split_axis=0, concat_axis=0, tiled=True)  21.9 us
    pallas_call x1, Pallas kernels, on_device(): pl.pallas_call(grad_kernel, out_shape=(jax.ShapeDtypeStruct((queries, qry...  19.9 us
    pallas_call x1, Pallas kernels, on_device(): pl.pallas_call(score_kernel, out_shape=(jax.ShapeDtypeStruct(block_shape,...  18.7 us
    all_to_all x4, starting transfers between devices, exchange(): return lax.all_to_all(array, axes, split_axis=0, concat_axis=0, tiled=True)  17.3 us
    all_to_all x1, blocking collectives, exchange(): return lax.all_to_all(array, axes, split_axis=0, concat_axis=0, tiled=True)  12.6 us
    dot_general x4, matrix products, on_device(): jnp.einsum('nhl,he->nle', s, projection, preferred_element_type=f32)  11 us
    ppermute x12, starting transfers between devices, swap(): return lax.ppermute(array, 'mp', [(i, i ^ bit) for i in range(groups)])  9.46 us
  transfers between devices with their start and end apart: 16, of which 7 were waited for; matrix products, arithmetic and copies ran while one was open for 19% of the time, Pallas kernels for 0%

profile of v3, /device:TPU:0, one launch (start us, length us, event | category | flops | bytes accessed | tf_op | source)
XLA Modules:
  0.0 180.8 jit_solution(15989519457741089393)
XLA Ops:
  1.5 0.9 fusion.34
  2.9 0.9 fusion.37
  3.9 3.2 %fusion.15 = bf16[32,128,128]{2,1,0:T(8,128)(2,1)} fusion(bf16[128,192,128]{2,1,0:T(8,128)(2,1)} %param.5, s32[]{:T(128)S(6)} %select_n.170, bf16[192,128]{1,0:T(8,128)(2,1)} %param.6), kind=kOutput, calls=%fused_computation.19 | convolution fusion | flops 201850880 | bytes 2670596 | tf_op jit(solution)/shard_map/nhl,he->nle/dot_general | solution.py:163
  7.6 2.2 %fusion.12 = bf16[32,128,128]{2,1,0:T(8,128)(2,1)S(1)} fusion(bf16[128,192,128]{2,1,0:T(8,128)(2,1)} %param.5, s32[]{:T(128)S(6)} %select_n.163, bf16[192,128]{1,0:T(8,128)(2,1)S(1)} %copy-done.2), kind=kOutput, calls=%fused_computation.18 | convolution fusion | flops 201850880 | bytes 2670596 | tf_op jit(solution)/shard_map/nhl,he->nle/dot_general | solution.py:163
  9.9 2.2 %fusion.4 = f32[32,128,128]{2,1,0:T(8,128)S(1)} fusion(bf16[128,192,128]{2,1,0:T(8,128)(2,1)} %param.5, s32[]{:T(128)S(6)} %select_n.169, bf16[192,128]{1,0:T(8,128)(2,1)S(1)} %copy-done.2), kind=kOutput, calls=%fused_computation.12 | convolution fusion | flops 201326592 | bytes 3719172 | tf_op jit(solution)/shard_map/nhl,he->nle/dot_general | solution.py:163
  12.2 3.0 %collective-permute-start.5 = (f32[2,32,128]{2,1,0:T(8,128)S(1)}, f32[2,32,128]{2,1,0:T(8,128)S(1)}, u32[]{:S(2)}, u32[]{:S(2)}) collective-permute-start(f32[2,32,128]{2,1,0:T(8,128)S(1)} %convolution_add_fusion), channel_id=1, source_target_pairs={{0,2},{1,3},{2,0},{3,1},{4,6},{5,7},{6,4},{7,5},{8,10},{9,11},{10,... | collective-permute-start | bytes 98312 | tf_op jit(solution)/shard_map/ppermute | solution.py:90
  15.4 1.7 collective-permute-done.5
  17.3 3.5 %add_convert_fusion = bf16[32,128,128]{2,1,0:T(8,128)(2,1)} fusion(bf16[32,128,128]{2,1,0:T(8,128)(2,1)} %collective-permute-done, bf16[128,192,128]{2,1,0:T(8,128)(2,1)} %param.5, s32[]{:T(128)S(6)} %select_n.162, bf16[192,128]{1,0:T(8,128)(2,1)S(1)} %copy-done.2), kind=kOutput, calls=%fused_computation.7 | convolution fusion | flops 202899456 | bytes 3719172 | tf_op jit(solution)/shard_map/nhl,he->nle/dot_general | solution.py:163
  21.5 6.4 %all-to-all-start = ((s32[32,1,128]{2,1,0:T(1,128)}), s32[32,1,128]{2,1,0:T(1,128)S(1)}, u32[]{:S(2)}, u32[]{:S(2)}) async-start(s32[32,1,128]{2,1,0:T(1,128)} %reshape.206), calls=%async_computation | async-start | bytes 32768 | tf_op jit(solution)/shard_map/all_to_all | solution.py:128
  28.0 1.8 %collective-permute-start.2 = (bf16[32,128,128]{2,1,0:T(8,128)(2,1)}, bf16[32,128,128]{2,1,0:T(8,128)(2,1)}, u32[]{:S(2)}, u32[]{:S(2)}) collective-permute-start(bf16[32,128,128]{2,1,0:T(8,128)(2,1)} %add_convert_fusion), channel_id=1, source_target_pairs={{0,2},{1,3},{2,0},{3,1},{4,6},{5,7},{6,4},{7,5},{8,10},{9,11},{10,... | collective-permute-start | bytes 3145736 | tf_op jit(solution)/shard_map/ppermute | solution.py:90
  29.8 5.2 %all-to-all-done = s32[32,1,128]{2,1,0:T(1,128)S(1)} async-done(((s32[32,1,128]{2,1,0:T(1,128)}), s32[32,1,128]{2,1,0:T(1,128)S(1)}, u32[]{:S(2)}, u32[]{:S(2)}) %all-to-all-start) | async-done | bytes 16416 | tf_op jit(solution)/shard_map/all_to_all | solution.py:128
  34.9 0.9 broadcast_in_dim.96
  35.9 2.6 %all-to-all-start.1 = ((bf16[32,2,32,128]{3,2,1,0:T(8,128)(2,1)}), bf16[32,2,32,128]{3,2,1,0:T(8,128)(2,1)S(1)}, u32[]{:S(2)}, u32[]{:S(2)}) async-start(bf16[32,2,32,128]{3,2,1,0:T(8,128)(2,1)} %broadcast_in_dim.96), calls=%async_computation.1 | async-start | bytes 1048576 | tf_op jit(solution)/shard_map/all_to_all | solution.py:128
  40.9 1.2 select_reduce_fusion.1
  43.4 15.2 %collective-permute-done.2 = bf16[32,128,128]{2,1,0:T(8,128)(2,1)} collective-permute-done((bf16[32,128,128]{2,1,0:T(8,128)(2,1)}, bf16[32,128,128]{2,1,0:T(8,128)(2,1)}, u32[]{:S(2)}, u32[]{:S(2)}) %collective-permute-start.2) | collective-permute-done | bytes 1048608 | tf_op jit(solution)/shard_map/ppermute | solution.py:90
  58.7 3.3 %convert_add_fusion.pre_ref = f32[32,128,128]{2,1,0:T(8,128)} fusion(bf16[32,128,128]{2,1,0:T(8,128)(2,1)} %collective-permute-done.2, f32[32,128,128]{2,1,0:T(8,128)S(1)} %fusion.4, bf16[32,128,128]{2,1,0:T(8,128)(2,1)} %collective-permute-done.1), kind=kLoop, calls=%fused_computation.6 | loop fusion | flops 2097152 | bytes 6291456 | tf_op jit(solution)/shard_map/add | solution.py:110
  62.8 18.7 %shard_map.75 = (bf16[32,128,128]{2,1,0:T(8,128)(2,1)}, f32[256,32,128]{2,1,0:T(8,128)}, f32[256,1,128]{2,1,0:T(1,128)}) custom-call(s32[256]{0:T(256)} %reshape.199.local_ref, s32[256]{0:T(256)} %fusion.60.query_ref, f32[32,128,128]{2,1,0:T(8,128)} %convert_add_fusion.pre_ref, bf16[64,32,128]{2,1,0:T(8,128)(2,1)} %bitcast.51), custom_call_target="tpu_custom_call" | custom-call | tf_op jit(solution)/shard_map/pallas_call | solution.py:188
  81.5 1.9 %slice_reduce_fusion = f32[256]{0:T(256)S(1)} fusion(f32[256,1,128]{2,1,0:T(1,128)} %get-tuple-element.13), kind=kLoop, calls=%fused_computation.38 | loop fusion | bytes 2048 | tf_op jit(solution)/shard_map/slice | solution.py:199
  83.7 12.6 %all_to_all.25 = f32[32,1,128]{2,1,0:T(1,128)S(1)} all-to-all(f32[32,1,128]{2,1,0:T(1,128)S(1)} %reshape.208), channel_id=1, replica_groups=mesh['dp'=8,'mp'=4] {'dp','mp'}, dimensions={0} | all-to-all | bytes 32768 | tf_op jit(solution)/shard_map/all_to_all | solution.py:128
  98.3 19.9 %shard_map.76 = (bf16[64,32,128]{2,1,0:T(8,128)(2,1)}, bf16[32,128,128]{2,1,0:T(8,128)(2,1)}) custom-call(s32[256]{0:T(256)} %reshape.199.local_ref, s32[256]{0:T(256)} %fusion.60.query_ref, f32[256]{0:T(256)} %subtract_select_fusion.grad_ref, f32[32,128,128]{2,1,0:T(8,128)} %convert_add_fusion.pre_ref, bf16[32,128,128]{2,1,0:T(8,128)(2,1)} %get-tuple-element.14.emb_ref, ...), custom_call_target="tpu_custom_call" | custom-call | tf_op jit(solution)/shard_map/pallas_call | solution.py:212
  118.1 2.7 %all-to-all-start.3 = ((bf16[32,2,32,128]{3,2,1,0:T(8,128)(2,1)}), bf16[32,2,32,128]{3,2,1,0:T(8,128)(2,1)S(1)}, u32[]{:S(2)}, u32[]{:S(2)}) async-start(bf16[32,2,32,128]{3,2,1,0:T(8,128)(2,1)} %bitcast.53), calls=%async_computation.3 | async-start | bytes 1048576 | tf_op jit(solution)/shard_map/all_to_all | solution.py:128
  120.9 1.7 collective-permute-start.9
  122.6 13.9 %all-to-all-done.3 = bf16[32,2,32,128]{3,2,1,0:T(8,128)(2,1)S(1)} async-done(((bf16[32,2,32,128]{3,2,1,0:T(8,128)(2,1)}), bf16[32,2,32,128]{3,2,1,0:T(8,128)(2,1)S(1)}, u32[]{:S(2)}, u32[]{:S(2)}) %all-to-all-start.3) | async-done | bytes 524320 | tf_op jit(solution)/shard_map/all_to_all | solution.py:128
  136.8 1.3 collective-permute-start.6
  138.1 13.8 %collective-permute-done.9 = bf16[32,128,128]{2,1,0:T(8,128)(2,1)S(1)} collective-permute-done((bf16[32,128,128]{2,1,0:T(8,128)(2,1)}, bf16[32,128,128]{2,1,0:T(8,128)(2,1)S(1)}, u32[]{:S(2)}, u32[]{:S(2)}) %collective-permute-start.9) | collective-permute-done | bytes 1048608 | tf_op jit(solution)/shard_map/ppermute | solution.py:90
  153.0 1.6 collective-permute-done.7
  154.8 1.4 broadcast_select_fusion.3
  156.8 2.3 %slice-done = s8[4194304]{0:T(1024)(128)(4,1)S(1)} async-done(((s8[6291456]{0:T(1024)(128)(4,1)}), s8[4194304]{0:T(1024)(128)(4,1)S(1)}, s32[]{:S(2)}) %slice-start) | async-done | bytes 4194328
  159.9 1.8 fusion.21
  162.5 5.6 %all-to-all-start.4 = ((bf16[8,192,128]{2,1,0:T(8,128)(2,1)}), bf16[8,192,128]{2,1,0:T(8,128)(2,1)S(1)}, u32[]{:S(2)}, u32[]{:S(2)}) async-start(bf16[8,192,128]{2,1,0:T(8,128)(2,1)} %broadcast_in_dim.104), calls=%async_computation.4 | async-start | bytes 786432 | tf_op jit(solution)/shard_map/all_to_all | solution.py:128
  169.0 8.2 %convolution_bitcast_fusion = f32[128,192,128]{2,1,0:T(8,128)} fusion(bf16[64,128,128]{2,1,0:T(8,128)(2,1)} %copy-done.1, bf16[64,128,128]{2,1,0:T(8,128)(2,1)S(1)} %get-tuple-element.24, bf16[192,128]{1,0:T(8,128)(2,1)S(1)} %copy-done.2), kind=kOutput, calls=%fused_computation.1 | convolution fusion | flops 807403520 | bytes 16826368 | tf_op jit(solution)/shard_map/nle,he->nhl/dot_general | solution.py:241
  177.2 2.9 %all-to-all-done.4 = bf16[8,192,128]{2,1,0:T(8,128)(2,1)S(1)} async-done(((bf16[8,192,128]{2,1,0:T(8,128)(2,1)}), bf16[8,192,128]{2,1,0:T(8,128)(2,1)S(1)}, u32[]{:S(2)}, u32[]{:S(2)}) %all-to-all-start.4) | async-done | bytes 393248 | tf_op jit(solution)/shard_map/all_to_all | solution.py:128
  (83 shorter events, 15.6 us)
Async XLA Ops:
  0.6 0.9 copy-start
  0.6 6.9 %copy-start.2 = (bf16[192,128]{1,0:T(8,128)(2,1)S(1)}, bf16[192,128]{1,0:T(8,128)(2,1)}, u32[]{:S(2)}) copy-start(bf16[192,128]{1,0:T(8,128)(2,1)} %param.6) | copy-start | bytes 147460
  2.5 9.6 %collective-permute-start.4 = (f32[2,32,128]{2,1,0:T(8,128)S(1)}, f32[2,32,128]{2,1,0:T(8,128)S(1)}, u32[]{:S(2)}, u32[]{:S(2)}) collective-permute-start(f32[2,32,128]{2,1,0:T(8,128)S(1)} %fusion.34), channel_id=1, source_target_pairs={{0,1},{1,0},{2,3},{3,2},{4,5},{5,4},{6,7},{7,6},{8,9},{9,8},{10,11... | collective-permute-start | bytes 98312 | tf_op jit(solution)/shard_map/ppermute | solution.py:90
  3.9 11.5 %collective-permute-start.3 = (f32[2,32,128]{2,1,0:T(8,128)S(1)}, f32[2,32,128]{2,1,0:T(8,128)S(1)}, u32[]{:S(2)}, u32[]{:S(2)}) collective-permute-start(f32[2,32,128]{2,1,0:T(8,128)S(1)} %fusion.37), channel_id=1, source_target_pairs={{0,1},{1,0},{2,3},{3,2},{4,5},{5,4},{6,7},{7,6},{8,9},{9,8},{10,11... | collective-permute-start | bytes 98312 | tf_op jit(solution)/shard_map/ppermute | solution.py:90
  7.1 36.3 %collective-permute-start.1 = (bf16[32,128,128]{2,1,0:T(8,128)(2,1)}, bf16[32,128,128]{2,1,0:T(8,128)(2,1)}, u32[]{:S(2)}, u32[]{:S(2)}) collective-permute-start(bf16[32,128,128]{2,1,0:T(8,128)(2,1)} %fusion.15), channel_id=1, source_target_pairs={{0,1},{1,0},{2,3},{3,2},{4,5},{5,4},{6,7},{7,6},{8,9},{9,8},{10,11... | collective-permute-start | bytes 3145736 | tf_op jit(solution)/shard_map/ppermute | solution.py:90
  9.8 7.6 %collective-permute-start = (bf16[32,128,128]{2,1,0:T(8,128)(2,1)S(1)}, bf16[32,128,128]{2,1,0:T(8,128)(2,1)}, u32[]{:S(2)}, u32[]{:S(2)}) collective-permute-start(bf16[32,128,128]{2,1,0:T(8,128)(2,1)S(1)} %fusion.12), channel_id=1, source_target_pairs={{0,1},{1,0},{2,3},{3,2},{4,5},{5,4},{6,7},{7,6},{8,9},{9,8},{10,11... | collective-permute-start | bytes 3145736 | tf_op jit(solution)/shard_map/ppermute | solution.py:90
  12.1 8.7 %copy-start.6 = (s32[2,64]{1,0:T(2,128)S(1)}, s32[2,64]{1,0:T(2,128)}, u32[]{:S(2)}) copy-start(s32[2,64]{1,0:T(2,128)} %param.7) | copy-start | bytes 1540
  12.2 4.8 %collective-permute-start.5 = (f32[2,32,128]{2,1,0:T(8,128)S(1)}, f32[2,32,128]{2,1,0:T(8,128)S(1)}, u32[]{:S(2)}, u32[]{:S(2)}) collective-permute-start(f32[2,32,128]{2,1,0:T(8,128)S(1)} %convolution_add_fusion), channel_id=1, source_target_pairs={{0,2},{1,3},{2,0},{3,1},{4,6},{5,7},{6,4},{7,5},{8,10},{9,11},{10,... | collective-permute-start | bytes 98312 | tf_op jit(solution)/shard_map/ppermute | solution.py:90
  21.5 13.5 %all-to-all-start = ((s32[32,1,128]{2,1,0:T(1,128)}), s32[32,1,128]{2,1,0:T(1,128)S(1)}, u32[]{:S(2)}, u32[]{:S(2)}) async-start(s32[32,1,128]{2,1,0:T(1,128)} %reshape.206), calls=%async_computation | async-start | bytes 32768 | tf_op jit(solution)/shard_map/all_to_all | solution.py:128
  28.0 30.7 %collective-permute-start.2 = (bf16[32,128,128]{2,1,0:T(8,128)(2,1)}, bf16[32,128,128]{2,1,0:T(8,128)(2,1)}, u32[]{:S(2)}, u32[]{:S(2)}) collective-permute-start(bf16[32,128,128]{2,1,0:T(8,128)(2,1)} %add_convert_fusion), channel_id=1, source_target_pairs={{0,2},{1,3},{2,0},{3,1},{4,6},{5,7},{6,4},{7,5},{8,10},{9,11},{10,... | collective-permute-start | bytes 3145736 | tf_op jit(solution)/shard_map/ppermute | solution.py:90
  35.9 26.1 %all-to-all-start.1 = ((bf16[32,2,32,128]{3,2,1,0:T(8,128)(2,1)}), bf16[32,2,32,128]{3,2,1,0:T(8,128)(2,1)S(1)}, u32[]{:S(2)}, u32[]{:S(2)}) async-start(bf16[32,2,32,128]{3,2,1,0:T(8,128)(2,1)} %broadcast_in_dim.96), calls=%async_computation.1 | async-start | bytes 1048576 | tf_op jit(solution)/shard_map/all_to_all | solution.py:128
  62.0 21.4 %copy-start.5 = (s32[256]{0:T(256)S(1)}, s32[256]{0:T(256)}, u32[]{:S(2)}) copy-start(s32[256]{0:T(256)} %fusion.60.query_ref) | copy-start | bytes 3076
  62.0 0.8 copy-start.3
  118.1 36.7 %copy-start.4 = (bf16[32,128,128]{2,1,0:T(8,128)(2,1)S(1)}, bf16[32,128,128]{2,1,0:T(8,128)(2,1)}, u32[]{:S(2)}) copy-start(bf16[32,128,128]{2,1,0:T(8,128)(2,1)} %get-tuple-element.17) | copy-start | bytes 3145732
  118.1 18.3 %all-to-all-start.3 = ((bf16[32,2,32,128]{3,2,1,0:T(8,128)(2,1)}), bf16[32,2,32,128]{3,2,1,0:T(8,128)(2,1)S(1)}, u32[]{:S(2)}, u32[]{:S(2)}) async-start(bf16[32,2,32,128]{3,2,1,0:T(8,128)(2,1)} %bitcast.53), calls=%async_computation.3 | async-start | bytes 1048576 | tf_op jit(solution)/shard_map/all_to_all | solution.py:128
  120.9 31.0 %collective-permute-start.9 = (bf16[32,128,128]{2,1,0:T(8,128)(2,1)}, bf16[32,128,128]{2,1,0:T(8,128)(2,1)S(1)}, u32[]{:S(2)}, u32[]{:S(2)}) collective-permute-start(bf16[32,128,128]{2,1,0:T(8,128)(2,1)} %get-tuple-element.17), channel_id=1, source_target_pairs={{0,2},{1,3},{2,0},{3,1},{4,6},{5,7},{6,4},{7,5},{8,10},{9,11},{10,... | collective-permute-start | bytes 3145736 | tf_op jit(solution)/shard_map/ppermute | solution.py:90
  122.6 32.2 %collective-permute-start.11 = (bf16[32,128,128]{2,1,0:T(8,128)(2,1)}, bf16[32,128,128]{2,1,0:T(8,128)(2,1)}, u32[]{:S(2)}, u32[]{:S(2)}) collective-permute-start(bf16[32,128,128]{2,1,0:T(8,128)(2,1)} %get-tuple-element.17), channel_id=1, source_target_pairs={{0,1},{1,0},{2,3},{3,2},{4,5},{5,4},{6,7},{7,6},{8,9},{9,8},{10,11... | collective-permute-start | bytes 3145736 | tf_op jit(solution)/shard_map/ppermute | solution.py:90
  136.7 16.3 %collective-permute-start.8 = (bf16[2,32,128]{2,1,0:T(8,128)(2,1)S(1)}, bf16[2,32,128]{2,1,0:T(8,128)(2,1)S(1)}, u32[]{:S(2)}, u32[]{:S(2)}) collective-permute-start(bf16[2,32,128]{2,1,0:T(8,128)(2,1)S(1)} %fusion.26), channel_id=1, source_target_pairs={{0,1},{1,0},{2,3},{3,2},{4,5},{5,4},{6,7},{7,6},{8,9},{9,8},{10,11... | collective-permute-start | bytes 49160 | tf_op jit(solution)/shard_map/ppermute | solution.py:90
  136.8 15.7 %collective-permute-start.6 = (bf16[2,32,128]{2,1,0:T(8,128)(2,1)S(1)}, bf16[2,32,128]{2,1,0:T(8,128)(2,1)S(1)}, u32[]{:S(2)}, u32[]{:S(2)}) collective-permute-start(bf16[2,32,128]{2,1,0:T(8,128)(2,1)S(1)} %fusion.26), channel_id=1, source_target_pairs={{0,2},{1,3},{2,0},{3,1},{4,6},{5,7},{6,4},{7,5},{8,10},{9,11},{10,... | collective-permute-start | bytes 49160 | tf_op jit(solution)/shard_map/ppermute | solution.py:90
  151.9 4.3 %collective-permute-start.10 = (bf16[32,128,128]{2,1,0:T(8,128)(2,1)S(1)}, bf16[32,128,128]{2,1,0:T(8,128)(2,1)S(1)}, u32[]{:S(2)}, u32[]{:S(2)}) collective-permute-start(bf16[32,128,128]{2,1,0:T(8,128)(2,1)S(1)} %collective-permute-done.9), channel_id=1, source_target_pairs={{0,1},{1,0},{2,3},{3,2},{4,5},{5,4},{6,7},{7,6},{8,9},{9,8},{10,11... | collective-permute-start | bytes 3145736 | tf_op jit(solution)/shard_map/ppermute | solution.py:90
  152.5 2.1 %collective-permute-start.7 = (bf16[2,32,128]{2,1,0:T(8,128)(2,1)S(1)}, bf16[2,32,128]{2,1,0:T(8,128)(2,1)S(1)}, u32[]{:S(2)}, u32[]{:S(2)}) collective-permute-start(bf16[2,32,128]{2,1,0:T(8,128)(2,1)S(1)} %collective-permute-done.6), channel_id=1, source_target_pairs={{0,1},{1,0},{2,3},{3,2},{4,5},{5,4},{6,7},{7,6},{8,9},{9,8},{10,11... | collective-permute-start | bytes 49160 | tf_op jit(solution)/shard_map/ppermute | solution.py:90
  156.2 2.9 %slice-start = ((s8[6291456]{0:T(1024)(128)(4,1)}), s8[4194304]{0:T(1024)(128)(4,1)S(1)}, s32[]{:S(2)}) async-start(s8[6291456]{0:T(1024)(128)(4,1)} %bitcast.49), calls=%async_computation.5 | async-start | bytes 8388608
  156.4 3.5 %slice-start.1 = ((s8[6291456]{0:T(1024)(128)(4,1)}), s8[2097152]{0:T(1024)(128)(4,1)S(1)}, s32[]{:S(2)}) async-start(s8[6291456]{0:T(1024)(128)(4,1)} %bitcast.49), calls=%async_computation.6 | async-start | bytes 4194304
  156.8 4.8 %copy-start.1 = (bf16[64,128,128]{2,1,0:T(8,128)(2,1)}, bf16[64,128,128]{2,1,0:T(8,128)(2,1)S(1)}, u32[]{:S(2)}) copy-start(bf16[64,128,128]{2,1,0:T(8,128)(2,1)S(1)} %get-tuple-element.25) | copy-start | bytes 6291460
  162.5 17.6 %all-to-all-start.4 = ((bf16[8,192,128]{2,1,0:T(8,128)(2,1)}), bf16[8,192,128]{2,1,0:T(8,128)(2,1)S(1)}, u32[]{:S(2)}, u32[]{:S(2)}) async-start(bf16[8,192,128]{2,1,0:T(8,128)(2,1)} %broadcast_in_dim.104), calls=%async_computation.4 | async-start | bytes 786432 | tf_op jit(solution)/shard_map/all_to_all | solution.py:128

commit v4 on v1

--- a/solution.py
+++ b/solution.py
@@ -1,3 +1,5 @@
+import functools
+
 import jax
 import jax.numpy as jnp
 from jax import lax
@@ -21,13 +23,18 @@
     return ((grad - unit * inner) / norm).astype(jnp.bfloat16)
 
 
+def unit_and_scale(pre):
+    scale = lax.rsqrt(jnp.sum(pre * pre, axis=-1, keepdims=True) + norm_eps)
+    return (pre * scale, scale)
+
+
 def score_kernel(local_ref, query_ref, pre_ref, visitors_ref, emb_ref, weights_ref, scores_ref):
     def embed(p, carry):
-        unit, _ = unit_rows(pre_ref[p])
+        unit, _ = unit_and_scale(pre_ref[p])
         emb_ref[p] = unit.astype(jnp.bfloat16)
         return carry
 
-    lax.fori_loop(0, pre_ref.shape[0], embed, 0)
+    lax.fori_loop(0, pre_ref.shape[0], embed, 0, unroll=4)
 
     def slots(b, carry):
         for u in range(BATCH):
@@ -41,7 +48,9 @@
             expo = jnp.exp(sharpness * sim)
             total = jnp.sum(expo, axis=-1, keepdims=True)
             weights_ref[s] = expo / total
-            score = jnp.sum(jnp.log(total), axis=0, keepdims=True) / sharpness
+            parts = [total[8 * i : 8 * i + 8] for i in range(total.shape[0] // 8)]
+            logs = [jnp.log(functools.reduce(jnp.multiply, parts[i : i + 4])) for i in range(0, len(parts), 4)]
+            score = jnp.sum(functools.reduce(jnp.add, logs), axis=0, keepdims=True) / sharpness
             scores_ref[s] = jnp.broadcast_to(score, scores_ref.shape[1:])
         return carry
 
@@ -79,11 +88,13 @@
     query_grad_ref[...] = query_sum[...].astype(jnp.bfloat16)
 
     def back(p, carry):
-        unit, norm = unit_rows(pre_ref[p])
-        pre_grad_ref[p] = unit_back(passage_sum[p], unit, norm)
-        return carry
-
-    lax.fori_loop(0, pre_ref.shape[0], back, 0)
+        unit, scale = unit_and_scale(pre_ref[p])
+        grad = passage_sum[p]
+        inner = jnp.sum(grad * unit, axis=-1, keepdims=True)
+        pre_grad_ref[p] = ((grad - unit * inner) * scale).astype(jnp.bfloat16)
+        return carry
+
+    lax.fori_loop(0, pre_ref.shape[0], back, 0, unroll=4)
 
 
 def swap(array, bit, groups):
@@ -102,8 +113,8 @@
         return lax.psum_scatter(project(states), "mp", scatter_dimension=0, tiled=True)
     far_out = swap(block(me ^ 3).astype(dtype), 1, groups)
     near_out = swap(block(me ^ 1).astype(dtype), 1, groups)
-    far = block(me ^ 2) + far_out.astype(f32)
-    far_in = swap(far.astype(dtype), 2, groups)
+    far = (block(me ^ 2) + far_out.astype(f32)).astype(dtype)
+    far_in = swap(far, 2, groups)
     return (block(me) + near_out.astype(f32)) + far_in.astype(f32)
 
 
@@ -146,7 +157,6 @@
     slot_total = owners * capacity
     queries = owners * query_rows
 
-    listings = spread(candidates, both, owners).reshape(owners, requests)
     query_pre = reduce_mp(
         query_states,
         lambda s: jnp.einsum("nlh,he->nle", s, projection, preferred_element_type=f32),
@@ -154,8 +164,17 @@
         f32,
     )
     query_unit, query_norm = unit_rows(query_pre)
-    visitors = spread(query_unit.astype(jnp.bfloat16), both, owners)
-    visitors = visitors.reshape(queries, qry_len, emb_dim)
+    id_rows = candidates.reshape(-1, emb_dim)
+    token_rows = query_rows * qry_len
+    message = jnp.concatenate(
+        [query_unit.astype(jnp.bfloat16).reshape(token_rows, emb_dim)]
+        + [part.astype(jnp.bfloat16) for part in (id_rows // 256, id_rows % 256)]
+    )
+    message = spread(message, both, owners).reshape(owners, -1, emb_dim)
+    visitors = message[:, :token_rows].reshape(queries, qry_len, emb_dim)
+    parts = message[:, token_rows:].astype(f32).astype(jnp.int32)
+    parts = parts.reshape(owners, 2, requests)
+    listings = parts[:, 0] * 256 + parts[:, 1]
     passage_pre = reduce_mp(
         passage_states,
         lambda s: jnp.einsum("nhl,he->nle", s, projection, preferred_element_type=f32),
@@ -231,10 +250,8 @@
     weight_part = weight_part + jnp.einsum(
         "nhl,nle->he", passage_states, passage_all, preferred_element_type=f32
     )
-    height = weight_part.shape[0] // replicas
-    pieces = exchange(weight_part.reshape(replicas, height, emb_dim), "dp")
-    piece = jnp.sum(pieces.reshape(replicas, height, emb_dim), axis=0)
-    weight_grad = spread(piece, "dp", replicas).reshape(weight_part.shape)
+    shares = spread(weight_part.astype(jnp.bfloat16), "dp", replicas)
+    weight_grad = jnp.sum(shares.reshape((replicas,) + weight_part.shape).astype(f32), axis=0)
     query_grads = jnp.einsum("nle,he->nlh", query_all, projection, preferred_element_type=f32)
     passage_grads = jnp.einsum("nle,he->nhl", passage_all, projection, preferred_element_type=f32)
     return (losses, weight_grad, query_grads, passage_grads)

time: 189 us -> 171 us (0.905)
  starting transfers between devices: 31.9 us -> 23.5 us
  Pallas kernels: 38.5 us -> 31.9 us
    all_to_all x5 -> x3, starting transfers between devices: 23.6 us -> 14.6 us  [exchange(): return lax.all_to_all(array, axes, split_axis=0, concat_axis=0, tiled=True)]
    pallas_call x1, Pallas kernels: 19.8 us -> 15.6 us  [on_device(): pl.pallas_call(grad_kernel, out_shape=(jax.ShapeDtypeStruct((queries, qry...]
    ppermute x12, waiting for transfers between devices: 36.3 us -> 32.1 us  [swap(): return lax.ppermute(array, 'mp', [(i, i ^ bit) for i in range(groups)])]
    all_to_all x5 -> x3, waiting for transfers between devices: 20.1 us -> 22.6 us  [exchange(): return lax.all_to_all(array, axes, split_axis=0, concat_axis=0, tiled=True)]
    pallas_call x1, Pallas kernels: 18.7 us -> 16.3 us  [on_device(): pl.pallas_call(score_kernel, out_shape=(jax.ShapeDtypeStruct(block_shape,...]
    unnamed x21 -> x18, local copies, waits for them, and re-layouts: 5.5 us -> 4.14 us
  transfers between devices with their start and end apart: 17 -> 15, of which waited for: 6 -> 7; matrix products, arithmetic and copies ran while one was open for 18% -> 18% of each run, Pallas kernels for 0% -> 0%
where the time goes in v4:
time: 171 us; the launch traced here: 170 us
  waiting for transfers between devices  54.7 us (32%)
  Pallas kernels  31.9 us (19%)
  matrix products  25.3 us (15%)
  starting transfers between devices  23.5 us (14%)
  blocking collectives  12.2 us (7%)
  local copies, waits for them, and re-layouts  10.9 us (6%)
  other arithmetic  10.6 us (6%)
    ppermute x12, waiting for transfers between devices, swap(): return lax.ppermute(array, 'mp', [(i, i ^ bit) for i in range(groups)])  32.1 us
    all_to_all x3, waiting for transfers between devices, exchange(): return lax.all_to_all(array, axes, split_axis=0, concat_axis=0, tiled=True)  22.6 us
    pallas_call x1, Pallas kernels, on_device(): pl.pallas_call(score_kernel, out_shape=(jax.ShapeDtypeStruct(block_shape,...  16.3 us
    pallas_call x1, Pallas kernels, on_device(): pl.pallas_call(grad_kernel, out_shape=(jax.ShapeDtypeStruct((queries, qry...  15.6 us
    all_to_all x3, starting transfers between devices, exchange(): return lax.all_to_all(array, axes, split_axis=0, concat_axis=0, tiled=True)  14.6 us
    all_to_all x1, blocking collectives, exchange(): return lax.all_to_all(array, axes, split_axis=0, concat_axis=0, tiled=True)  12.2 us
    dot_general x4, matrix products, on_device(): jnp.einsum('nhl,he->nle', s, projection, preferred_element_type=f32)  12 us
    ppermute x12, starting transfers between devices, swap(): return lax.ppermute(array, 'mp', [(i, i ^ bit) for i in range(groups)])  8.98 us
  transfers between devices with their start and end apart: 15, of which 7 were waited for; matrix products, arithmetic and copies ran while one was open for 18% of the time, Pallas kernels for 0%

profile of v4, /device:TPU:0, one launch (start us, length us, event | category | flops | bytes accessed | tf_op | source)
XLA Modules:
  0.0 170.0 jit_solution(10698120508648874447)
XLA Ops:
  1.6 0.9 fusion.38
  3.0 0.9 fusion.41
  4.0 3.2 %fusion.15 = bf16[32,128,128]{2,1,0:T(8,128)(2,1)} fusion(bf16[128,192,128]{2,1,0:T(8,128)(2,1)} %param.5, s32[]{:T(128)S(6)} %select_n.194, bf16[192,128]{1,0:T(8,128)(2,1)} %param.6), kind=kOutput, calls=%fused_computation.19 | convolution fusion | flops 201850880 | bytes 2670596 | tf_op jit(solution)/shard_map/nhl,he->nle/dot_general | solution.py:180
  7.8 2.5 %collective-permute-start.2 = (f32[2,32,128]{2,1,0:T(8,128)S(1)}, f32[2,32,128]{2,1,0:T(8,128)S(1)}, u32[]{:S(2)}, u32[]{:S(2)}) collective-permute-start(f32[2,32,128]{2,1,0:T(8,128)S(1)} %convolution_add_fusion), channel_id=1, source_target_pairs={{0,2},{1,3},{2,0},{3,1},{4,6},{5,7},{6,4},{7,5},{8,10},{9,11},{10,... | collective-permute-start | bytes 98312 | tf_op jit(solution)/shard_map/ppermute | solution.py:101
  10.3 2.0 %collective-permute-done.2 = f32[2,32,128]{2,1,0:T(8,128)S(1)} collective-permute-done((f32[2,32,128]{2,1,0:T(8,128)S(1)}, f32[2,32,128]{2,1,0:T(8,128)S(1)}, u32[]{:S(2)}, u32[]{:S(2)}) %collective-permute-start.2) | collective-permute-done | bytes 32800 | tf_op jit(solution)/shard_map/ppermute | solution.py:101
  12.7 0.9 broadcast_in_dim.88
  13.6 6.2 %all-to-all-start = ((bf16[32,66,128]{2,1,0:T(8,128)(2,1)}), bf16[32,66,128]{2,1,0:T(8,128)(2,1)S(1)}, u32[]{:S(2)}, u32[]{:S(2)}) async-start(bf16[32,66,128]{2,1,0:T(8,128)(2,1)} %broadcast_in_dim.88), calls=%async_computation | async-start | bytes 1179648 | tf_op jit(solution)/shard_map/all_to_all | solution.py:136
  19.8 3.2 %fusion.10 = bf16[32,128,128]{2,1,0:T(8,128)(2,1)} fusion(bf16[128,192,128]{2,1,0:T(8,128)(2,1)} %param.5, s32[]{:T(128)S(6)} %select_n.192, bf16[192,128]{1,0:T(8,128)(2,1)S(1)} %copy-done.2), kind=kOutput, calls=%fused_computation.18 | convolution fusion | flops 201850880 | bytes 2670596 | tf_op jit(solution)/shard_map/nhl,he->nle/dot_general | solution.py:180
  23.4 2.2 %fusion.8 = f32[32,128,128]{2,1,0:T(8,128)S(1)} fusion(bf16[128,192,128]{2,1,0:T(8,128)(2,1)} %param.5, s32[]{:T(128)S(6)} %select_n.191, bf16[192,128]{1,0:T(8,128)(2,1)S(1)} %copy-done.2), kind=kOutput, calls=%fused_computation.16 | convolution fusion | flops 201326592 | bytes 3719172 | tf_op jit(solution)/shard_map/nhl,he->nle/dot_general | solution.py:180
  25.6 3.5 %add_convert_fusion = bf16[32,128,128]{2,1,0:T(8,128)(2,1)} fusion(bf16[32,128,128]{2,1,0:T(8,128)(2,1)} %collective-permute-done.4, bf16[128,192,128]{2,1,0:T(8,128)(2,1)} %param.5, s32[]{:T(128)S(6)} %select_n.193, bf16[192,128]{1,0:T(8,128)(2,1)S(1)} %copy-done.2), kind=kOutput, calls=%fused_computation.7 | convolution fusion | flops 202899456 | bytes 3719172 | tf_op jit(solution)/shard_map/nhl,he->nle/dot_general | solution.py:180
  29.1 1.7 collective-permute-start.5
  30.8 5.8 %all-to-all-done = bf16[32,66,128]{2,1,0:T(8,128)(2,1)S(1)} async-done(((bf16[32,66,128]{2,1,0:T(8,128)(2,1)}), bf16[32,66,128]{2,1,0:T(8,128)(2,1)S(1)}, u32[]{:S(2)}, u32[]{:S(2)}) %all-to-all-start) | async-done | bytes 540704 | tf_op jit(solution)/shard_map/all_to_all | solution.py:136
  37.7 1.2 select_reduce_fusion.1
  41.1 14.7 %collective-permute-done.5 = bf16[32,128,128]{2,1,0:T(8,128)(2,1)} collective-permute-done((bf16[32,128,128]{2,1,0:T(8,128)(2,1)}, bf16[32,128,128]{2,1,0:T(8,128)(2,1)}, u32[]{:S(2)}, u32[]{:S(2)}) %collective-permute-start.5) | collective-permute-done | bytes 1048608 | tf_op jit(solution)/shard_map/ppermute | solution.py:101
  55.7 3.3 %convert_add_fusion.pre_ref = f32[32,128,128]{2,1,0:T(8,128)} fusion(bf16[32,128,128]{2,1,0:T(8,128)(2,1)} %collective-permute-done.5, f32[32,128,128]{2,1,0:T(8,128)S(1)} %fusion.8, bf16[32,128,128]{2,1,0:T(8,128)(2,1)} %collective-permute-done.3), kind=kLoop, calls=%fused_computation.6 | loop fusion | flops 2097152 | bytes 6291456 | tf_op jit(solution)/shard_map/add | solution.py:118
  59.1 16.3 %shard_map.75 = (bf16[32,128,128]{2,1,0:T(8,128)(2,1)}, f32[256,32,128]{2,1,0:T(8,128)}, f32[256,1,128]{2,1,0:T(1,128)}) custom-call(s32[256]{0:T(256)} %reshape.271.local_ref, s32[256]{0:T(256)} %fusion.62.query_ref, f32[32,128,128]{2,1,0:T(8,128)} %convert_add_fusion.pre_ref, bf16[64,32,128]{2,1,0:T(8,128)(2,1)} %bitcast.57), custom_call_target="tpu_custom_call" | custom-call | tf_op jit(solution)/shard_map/pallas_call | solution.py:203
  75.3 1.9 %slice_reduce_fusion = f32[256]{0:T(256)S(1)} fusion(f32[256,1,128]{2,1,0:T(1,128)} %get-tuple-element.9), kind=kLoop, calls=%fused_computation.38 | loop fusion | bytes 2048 | tf_op jit(solution)/shard_map/slice | solution.py:214
  77.5 12.2 %all_to_all.20 = f32[32,1,128]{2,1,0:T(1,128)S(1)} all-to-all(f32[32,1,128]{2,1,0:T(1,128)S(1)} %reshape.278), channel_id=1, replica_groups=mesh['dp'=8,'mp'=4] {'dp','mp'}, dimensions={0} | all-to-all | bytes 32768 | tf_op jit(solution)/shard_map/all_to_all | solution.py:136
  91.8 15.6 %shard_map.76 = (bf16[64,32,128]{2,1,0:T(8,128)(2,1)}, bf16[32,128,128]{2,1,0:T(8,128)(2,1)}) custom-call(s32[256]{0:T(256)} %reshape.271.local_ref, s32[256]{0:T(256)} %fusion.62.query_ref, f32[256]{0:T(256)} %subtract_select_fusion.grad_ref, f32[32,128,128]{2,1,0:T(8,128)} %convert_add_fusion.pre_ref, bf16[32,128,128]{2,1,0:T(8,128)(2,1)} %get-tuple-element.10.emb_ref, ...), custom_call_target="tpu_custom_call" | custom-call | tf_op jit(solution)/shard_map/pallas_call | solution.py:227
  107.4 2.7 %all-to-all-start.2 = ((bf16[32,2,32,128]{3,2,1,0:T(8,128)(2,1)}), bf16[32,2,32,128]{3,2,1,0:T(8,128)(2,1)S(1)}, u32[]{:S(2)}, u32[]{:S(2)}) async-start(bf16[32,2,32,128]{3,2,1,0:T(8,128)(2,1)} %bitcast.59), calls=%async_computation.2 | async-start | bytes 1048576 | tf_op jit(solution)/shard_map/all_to_all | solution.py:136
  110.1 1.7 %collective-permute-start.9 = (bf16[32,128,128]{2,1,0:T(8,128)(2,1)}, bf16[32,128,128]{2,1,0:T(8,128)(2,1)S(1)}, u32[]{:S(2)}, u32[]{:S(2)}) collective-permute-start(bf16[32,128,128]{2,1,0:T(8,128)(2,1)} %get-tuple-element.13), channel_id=1, source_target_pairs={{0,2},{1,3},{2,0},{3,1},{4,6},{5,7},{6,4},{7,5},{8,10},{9,11},{10,... | collective-permute-start | bytes 3145736 | tf_op jit(solution)/shard_map/ppermute | solution.py:101
  111.8 13.9 %all-to-all-done.2 = bf16[32,2,32,128]{3,2,1,0:T(8,128)(2,1)S(1)} async-done(((bf16[32,2,32,128]{3,2,1,0:T(8,128)(2,1)}), bf16[32,2,32,128]{3,2,1,0:T(8,128)(2,1)S(1)}, u32[]{:S(2)}, u32[]{:S(2)}) %all-to-all-start.2) | async-done | bytes 524320 | tf_op jit(solution)/shard_map/all_to_all | solution.py:136
  126.0 1.3 collective-permute-start.6
  127.3 13.8 %collective-permute-done.9 = bf16[32,128,128]{2,1,0:T(8,128)(2,1)S(1)} collective-permute-done((bf16[32,128,128]{2,1,0:T(8,128)(2,1)}, bf16[32,128,128]{2,1,0:T(8,128)(2,1)S(1)}, u32[]{:S(2)}, u32[]{:S(2)}) %collective-permute-start.9) | collective-permute-done | bytes 1048608 | tf_op jit(solution)/shard_map/ppermute | solution.py:101
  142.2 1.6 collective-permute-done.7
  144.1 1.4 broadcast_select_fusion.3
  146.1 2.3 %slice-done = s8[4194304]{0:T(1024)(128)(4,1)S(1)} async-done(((s8[6291456]{0:T(1024)(128)(4,1)}), s8[4194304]{0:T(1024)(128)(4,1)S(1)}, s32[]{:S(2)}) %slice-start) | async-done | bytes 4194328
  149.1 1.8 %fusion.21 = bf16[192,128]{1,0:T(8,128)(2,1)S(1)} fusion(f32[128,192]{0,1:T(8,128)S(1)} %convolution_bitcast_fusion.1, bf16[128,192,128]{2,1,0:T(8,128)(2,1)S(1)} %bitcast.56, bf16[64,128,128]{2,1,0:T(8,128)(2,1)S(1)} %get-tuple-element.21, bf16[64,128,128]{2,1,0:T(8,128)(2,1)S(1)} %get-tuple-element.20), kind=kOutput, calls=%fused_computation.24 | convolution fusion | flops 807452672 | bytes 10633216 | tf_op jit(solution)/shard_map/nhl,nle->he/dot_general | solution.py:250
  151.7 5.6 %all-to-all-start.3 = ((bf16[8,192,128]{2,1,0:T(8,128)(2,1)}), bf16[8,192,128]{2,1,0:T(8,128)(2,1)S(1)}, u32[]{:S(2)}, u32[]{:S(2)}) async-start(bf16[8,192,128]{2,1,0:T(8,128)(2,1)} %broadcast_in_dim.100), calls=%async_computation.3 | async-start | bytes 786432 | tf_op jit(solution)/shard_map/all_to_all | solution.py:136
  157.4 0.9 fusion.32
  158.3 8.2 %convolution_bitcast_fusion = f32[128,192,128]{2,1,0:T(8,128)} fusion(bf16[64,128,128]{2,1,0:T(8,128)(2,1)} %copy-done.1, bf16[64,128,128]{2,1,0:T(8,128)(2,1)S(1)} %get-tuple-element.20, bf16[192,128]{1,0:T(8,128)(2,1)S(1)} %copy-done.2), kind=kOutput, calls=%fused_computation.1 | convolution fusion | flops 807403520 | bytes 16826368 | tf_op jit(solution)/shard_map/nle,he->nhl/dot_general | solution.py:256
  166.4 2.9 %all-to-all-done.3 = bf16[8,192,128]{2,1,0:T(8,128)(2,1)S(1)} async-done(((bf16[8,192,128]{2,1,0:T(8,128)(2,1)}), bf16[8,192,128]{2,1,0:T(8,128)(2,1)S(1)}, u32[]{:S(2)}, u32[]{:S(2)}) %all-to-all-start.3) | async-done | bytes 393248 | tf_op jit(solution)/shard_map/all_to_all | solution.py:136
  (79 shorter events, 12.9 us)
Async XLA Ops:
  0.6 0.9 copy-start
  0.6 7.0 %copy-start.2 = (bf16[192,128]{1,0:T(8,128)(2,1)S(1)}, bf16[192,128]{1,0:T(8,128)(2,1)}, u32[]{:S(2)}) copy-start(bf16[192,128]{1,0:T(8,128)(2,1)} %param.6) | copy-start | bytes 147460
  0.7 6.9 %copy-start.5 = (s32[2,64]{1,0:T(2,128)S(1)}, s32[2,64]{1,0:T(2,128)}, u32[]{:S(2)}) copy-start(s32[2,64]{1,0:T(2,128)} %param.7) | copy-start | bytes 1540
  2.5 5.2 %collective-permute-start.1 = (f32[2,32,128]{2,1,0:T(8,128)S(1)}, f32[2,32,128]{2,1,0:T(8,128)S(1)}, u32[]{:S(2)}, u32[]{:S(2)}) collective-permute-start(f32[2,32,128]{2,1,0:T(8,128)S(1)} %fusion.38), channel_id=1, source_target_pairs={{0,1},{1,0},{2,3},{3,2},{4,5},{5,4},{6,7},{7,6},{8,9},{9,8},{10,11... | collective-permute-start | bytes 98312 | tf_op jit(solution)/shard_map/ppermute | solution.py:101
  3.9 6.4 %collective-permute-start = (f32[2,32,128]{2,1,0:T(8,128)S(1)}, f32[2,32,128]{2,1,0:T(8,128)S(1)}, u32[]{:S(2)}, u32[]{:S(2)}) collective-permute-start(f32[2,32,128]{2,1,0:T(8,128)S(1)} %fusion.41), channel_id=1, source_target_pairs={{0,1},{1,0},{2,3},{3,2},{4,5},{5,4},{6,7},{7,6},{8,9},{9,8},{10,11... | collective-permute-start | bytes 98312 | tf_op jit(solution)/shard_map/ppermute | solution.py:101
  7.1 18.5 %collective-permute-start.4 = (bf16[32,128,128]{2,1,0:T(8,128)(2,1)}, bf16[32,128,128]{2,1,0:T(8,128)(2,1)}, u32[]{:S(2)}, u32[]{:S(2)}) collective-permute-start(bf16[32,128,128]{2,1,0:T(8,128)(2,1)} %fusion.15), channel_id=1, source_target_pairs={{0,1},{1,0},{2,3},{3,2},{4,5},{5,4},{6,7},{7,6},{8,9},{9,8},{10,11... | collective-permute-start | bytes 3145736 | tf_op jit(solution)/shard_map/ppermute | solution.py:101
  7.8 4.6 %collective-permute-start.2 = (f32[2,32,128]{2,1,0:T(8,128)S(1)}, f32[2,32,128]{2,1,0:T(8,128)S(1)}, u32[]{:S(2)}, u32[]{:S(2)}) collective-permute-start(f32[2,32,128]{2,1,0:T(8,128)S(1)} %convolution_add_fusion), channel_id=1, source_target_pairs={{0,2},{1,3},{2,0},{3,1},{4,6},{5,7},{6,4},{7,5},{8,10},{9,11},{10,... | collective-permute-start | bytes 98312 | tf_op jit(solution)/shard_map/ppermute | solution.py:101
  13.6 23.0 %all-to-all-start = ((bf16[32,66,128]{2,1,0:T(8,128)(2,1)}), bf16[32,66,128]{2,1,0:T(8,128)(2,1)S(1)}, u32[]{:S(2)}, u32[]{:S(2)}) async-start(bf16[32,66,128]{2,1,0:T(8,128)(2,1)} %broadcast_in_dim.88), calls=%async_computation | async-start | bytes 1179648 | tf_op jit(solution)/shard_map/all_to_all | solution.py:136
  23.0 18.0 %collective-permute-start.3 = (bf16[32,128,128]{2,1,0:T(8,128)(2,1)}, bf16[32,128,128]{2,1,0:T(8,128)(2,1)}, u32[]{:S(2)}, u32[]{:S(2)}) collective-permute-start(bf16[32,128,128]{2,1,0:T(8,128)(2,1)} %fusion.10), channel_id=1, source_target_pairs={{0,1},{1,0},{2,3},{3,2},{4,5},{5,4},{6,7},{7,6},{8,9},{9,8},{10,11... | collective-permute-start | bytes 3145736 | tf_op jit(solution)/shard_map/ppermute | solution.py:101
  29.1 26.7 %collective-permute-start.5 = (bf16[32,128,128]{2,1,0:T(8,128)(2,1)}, bf16[32,128,128]{2,1,0:T(8,128)(2,1)}, u32[]{:S(2)}, u32[]{:S(2)}) collective-permute-start(bf16[32,128,128]{2,1,0:T(8,128)(2,1)} %add_convert_fusion), channel_id=1, source_target_pairs={{0,2},{1,3},{2,0},{3,1},{4,6},{5,7},{6,4},{7,5},{8,10},{9,11},{10,... | collective-permute-start | bytes 3145736 | tf_op jit(solution)/shard_map/ppermute | solution.py:101
  59.0 18.2 %copy-start.4 = (s32[256]{0:T(256)S(1)}, s32[256]{0:T(256)}, u32[]{:S(2)}) copy-start(s32[256]{0:T(256)} %fusion.62.query_ref) | copy-start | bytes 3076
  107.4 36.7 %copy-start.3 = (bf16[32,128,128]{2,1,0:T(8,128)(2,1)S(1)}, bf16[32,128,128]{2,1,0:T(8,128)(2,1)}, u32[]{:S(2)}) copy-start(bf16[32,128,128]{2,1,0:T(8,128)(2,1)} %get-tuple-element.13) | copy-start | bytes 3145732
  107.4 18.3 %all-to-all-start.2 = ((bf16[32,2,32,128]{3,2,1,0:T(8,128)(2,1)}), bf16[32,2,32,128]{3,2,1,0:T(8,128)(2,1)S(1)}, u32[]{:S(2)}, u32[]{:S(2)}) async-start(bf16[32,2,32,128]{3,2,1,0:T(8,128)(2,1)} %bitcast.59), calls=%async_computation.2 | async-start | bytes 1048576 | tf_op jit(solution)/shard_map/all_to_all | solution.py:136
  110.1 31.0 %collective-permute-start.9 = (bf16[32,128,128]{2,1,0:T(8,128)(2,1)}, bf16[32,128,128]{2,1,0:T(8,128)(2,1)S(1)}, u32[]{:S(2)}, u32[]{:S(2)}) collective-permute-start(bf16[32,128,128]{2,1,0:T(8,128)(2,1)} %get-tuple-element.13), channel_id=1, source_target_pairs={{0,2},{1,3},{2,0},{3,1},{4,6},{5,7},{6,4},{7,5},{8,10},{9,11},{10,... | collective-permute-start | bytes 3145736 | tf_op jit(solution)/shard_map/ppermute | solution.py:101
  111.8 32.2 %collective-permute-start.11 = (bf16[32,128,128]{2,1,0:T(8,128)(2,1)}, bf16[32,128,128]{2,1,0:T(8,128)(2,1)}, u32[]{:S(2)}, u32[]{:S(2)}) collective-permute-start(bf16[32,128,128]{2,1,0:T(8,128)(2,1)} %get-tuple-element.13), channel_id=1, source_target_pairs={{0,1},{1,0},{2,3},{3,2},{4,5},{5,4},{6,7},{7,6},{8,9},{9,8},{10,11... | collective-permute-start | bytes 3145736 | tf_op jit(solution)/shard_map/ppermute | solution.py:101
  126.0 16.3 %collective-permute-start.8 = (bf16[2,32,128]{2,1,0:T(8,128)(2,1)S(1)}, bf16[2,32,128]{2,1,0:T(8,128)(2,1)S(1)}, u32[]{:S(2)}, u32[]{:S(2)}) collective-permute-start(bf16[2,32,128]{2,1,0:T(8,128)(2,1)S(1)} %fusion.26), channel_id=1, source_target_pairs={{0,1},{1,0},{2,3},{3,2},{4,5},{5,4},{6,7},{7,6},{8,9},{9,8},{10,11... | collective-permute-start | bytes 49160 | tf_op jit(solution)/shard_map/ppermute | solution.py:101
  126.0 15.7 %collective-permute-start.6 = (bf16[2,32,128]{2,1,0:T(8,128)(2,1)S(1)}, bf16[2,32,128]{2,1,0:T(8,128)(2,1)S(1)}, u32[]{:S(2)}, u32[]{:S(2)}) collective-permute-start(bf16[2,32,128]{2,1,0:T(8,128)(2,1)S(1)} %fusion.26), channel_id=1, source_target_pairs={{0,2},{1,3},{2,0},{3,1},{4,6},{5,7},{6,4},{7,5},{8,10},{9,11},{10,... | collective-permute-start | bytes 49160 | tf_op jit(solution)/shard_map/ppermute | solution.py:101
  141.1 4.3 %collective-permute-start.10 = (bf16[32,128,128]{2,1,0:T(8,128)(2,1)S(1)}, bf16[32,128,128]{2,1,0:T(8,128)(2,1)S(1)}, u32[]{:S(2)}, u32[]{:S(2)}) collective-permute-start(bf16[32,128,128]{2,1,0:T(8,128)(2,1)S(1)} %collective-permute-done.9), channel_id=1, source_target_pairs={{0,1},{1,0},{2,3},{3,2},{4,5},{5,4},{6,7},{7,6},{8,9},{9,8},{10,11... | collective-permute-start | bytes 3145736 | tf_op jit(solution)/shard_map/ppermute | solution.py:101
  141.7 2.1 %collective-permute-start.7 = (bf16[2,32,128]{2,1,0:T(8,128)(2,1)S(1)}, bf16[2,32,128]{2,1,0:T(8,128)(2,1)S(1)}, u32[]{:S(2)}, u32[]{:S(2)}) collective-permute-start(bf16[2,32,128]{2,1,0:T(8,128)(2,1)S(1)} %collective-permute-done.6), channel_id=1, source_target_pairs={{0,1},{1,0},{2,3},{3,2},{4,5},{5,4},{6,7},{7,6},{8,9},{9,8},{10,11... | collective-permute-start | bytes 49160 | tf_op jit(solution)/shard_map/ppermute | solution.py:101
  145.5 2.9 %slice-start = ((s8[6291456]{0:T(1024)(128)(4,1)}), s8[4194304]{0:T(1024)(128)(4,1)S(1)}, s32[]{:S(2)}) async-start(s8[6291456]{0:T(1024)(128)(4,1)} %bitcast.55), calls=%async_computation.4 | async-start | bytes 8388608
  145.6 3.5 %slice-start.1 = ((s8[6291456]{0:T(1024)(128)(4,1)}), s8[2097152]{0:T(1024)(128)(4,1)S(1)}, s32[]{:S(2)}) async-start(s8[6291456]{0:T(1024)(128)(4,1)} %bitcast.55), calls=%async_computation.5 | async-start | bytes 4194304
  146.1 4.8 %copy-start.1 = (bf16[64,128,128]{2,1,0:T(8,128)(2,1)}, bf16[64,128,128]{2,1,0:T(8,128)(2,1)S(1)}, u32[]{:S(2)}) copy-start(bf16[64,128,128]{2,1,0:T(8,128)(2,1)S(1)} %get-tuple-element.21) | copy-start | bytes 6291460
  151.7 17.6 %all-to-all-start.3 = ((bf16[8,192,128]{2,1,0:T(8,128)(2,1)}), bf16[8,192,128]{2,1,0:T(8,128)(2,1)S(1)}, u32[]{:S(2)}, u32[]{:S(2)}) async-start(bf16[8,192,128]{2,1,0:T(8,128)(2,1)} %broadcast_in_dim.100), calls=%async_computation.3 | async-start | bytes 786432 | tf_op jit(solution)/shard_map/all_to_all | solution.py:136

commit v5 on v4

--- a/solution.py
+++ b/solution.py
@@ -101,7 +101,7 @@
     return lax.ppermute(array, "mp", [(i, i ^ bit) for i in range(groups)])
 
 
-def reduce_mp(states, project, groups, dtype):
+def reduce_mp(states, project, groups, dtype, later=None):
     f32 = jnp.float32
     me = lax.axis_index("mp")
     rows = states.shape[0] // groups
@@ -110,12 +110,16 @@
         return project(lax.dynamic_slice_in_dim(states, index * rows, rows, 0))
 
     if groups != 4:
-        return lax.psum_scatter(project(states), "mp", scatter_dimension=0, tiled=True)
+        whole = lax.psum_scatter(project(states), "mp", scatter_dimension=0, tiled=True)
+        return whole, later
     far_out = swap(block(me ^ 3).astype(dtype), 1, groups)
     near_out = swap(block(me ^ 1).astype(dtype), 1, groups)
     far = (block(me ^ 2) + far_out.astype(f32)).astype(dtype)
     far_in = swap(far, 2, groups)
-    return (block(me) + near_out.astype(f32)) + far_in.astype(f32)
+    near = block(me) + near_out.astype(f32)
+    if later is not None:
+        near, later = lax.optimization_barrier((near, later))
+    return near + far_in.astype(f32), later
 
 
 def gather_mp(mine, groups):
@@ -157,7 +161,7 @@
     slot_total = owners * capacity
     queries = owners * query_rows
 
-    query_pre = reduce_mp(
+    query_pre, _ = reduce_mp(
         query_states,
         lambda s: jnp.einsum("nlh,he->nle", s, projection, preferred_element_type=f32),
         groups,
@@ -170,18 +174,18 @@
         [query_unit.astype(jnp.bfloat16).reshape(token_rows, emb_dim)]
         + [part.astype(jnp.bfloat16) for part in (id_rows // 256, id_rows % 256)]
     )
+    passage_pre, message = reduce_mp(
+        passage_states,
+        lambda s: jnp.einsum("nhl,he->nle", s, projection, preferred_element_type=f32),
+        groups,
+        jnp.bfloat16,
+        message,
+    )
     message = spread(message, both, owners).reshape(owners, -1, emb_dim)
     visitors = message[:, :token_rows].reshape(queries, qry_len, emb_dim)
     parts = message[:, token_rows:].astype(f32).astype(jnp.int32)
     parts = parts.reshape(owners, 2, requests)
     listings = parts[:, 0] * 256 + parts[:, 1]
-    passage_pre = reduce_mp(
-        passage_states,
-        lambda s: jnp.einsum("nhl,he->nle", s, projection, preferred_element_type=f32),
-        groups,
-        jnp.bfloat16,
-    )
-
     held = (listings // passage_rows) == me
     within = jnp.cumsum(held.astype(jnp.int32), axis=1) - 1
     chosen = held[:, None, :] & (

time: 171 us -> 171 us (level)
  waiting for transfers between devices: 54.7 us -> 56.8 us
    all_to_all x3, waiting for transfers between devices: 22.6 us -> 28.1 us  [exchange(): return lax.all_to_all(array, axes, split_axis=0, concat_axis=0, tiled=True)]
    ppermute x12, waiting for transfers between devices: 32.1 us -> 28.7 us  [swap(): return lax.ppermute(array, 'mp', [(i, i ^ bit) for i in range(groups)])]
  transfers between devices with their start and end apart: 15 -> 15, of which waited for: 7 -> 7; matrix products, arithmetic and copies ran while one was open for 18% -> 17% of each run, Pallas kernels for 0% -> 0%
where the time goes in v5:
time: 171 us; the launch traced here: 170 us
  waiting for transfers between devices  56.8 us (33%)
  Pallas kernels  31.9 us (19%)
  matrix products  24.3 us (14%)
  starting transfers between devices  24.1 us (14%)
  blocking collectives  11.2 us (7%)
  local copies, waits for them, and re-layouts  10.9 us (6%)
  other arithmetic  10.2 us (6%)
    ppermute x12, waiting for transfers between devices, swap(): return lax.ppermute(array, 'mp', [(i, i ^ bit) for i in range(groups)])  28.7 us
    all_to_all x3, waiting for transfers between devices, exchange(): return lax.all_to_all(array, axes, split_axis=0, concat_axis=0, tiled=True)  28.1 us
    pallas_call x1, Pallas kernels, on_device(): pl.pallas_call(score_kernel, out_shape=(jax.ShapeDtypeStruct(block_shape,...  16.3 us
    pallas_call x1, Pallas kernels, on_device(): pl.pallas_call(grad_kernel, out_shape=(jax.ShapeDtypeStruct((queries, qry...  15.6 us
    all_to_all x3, starting transfers between devices, exchange(): return lax.all_to_all(array, axes, split_axis=0, concat_axis=0, tiled=True)  14.7 us
    all_to_all x1, blocking collectives, exchange(): return lax.all_to_all(array, axes, split_axis=0, concat_axis=0, tiled=True)  11.2 us
    dot_general x4, matrix products, on_device(): jnp.einsum('nhl,he->nle', s, projection, preferred_element_type=f32)  11 us
    ppermute x12, starting transfers between devices, swap(): return lax.ppermute(array, 'mp', [(i, i ^ bit) for i in range(groups)])  9.39 us
  transfers between devices with their start and end apart: 15, of which 7 were waited for; matrix products, arithmetic and copies ran while one was open for 17% of the time, Pallas kernels for 0%

profile of v5, /device:TPU:0, one launch (start us, length us, event | category | flops | bytes accessed | tf_op | source)
XLA Modules:
  0.0 170.2 jit_solution(13196416252203592352)
XLA Ops:
  1.5 0.9 fusion.38
  2.9 0.9 fusion.41
  3.9 3.2 %fusion.17 = bf16[32,128,128]{2,1,0:T(8,128)(2,1)} fusion(bf16[128,192,128]{2,1,0:T(8,128)(2,1)} %param.5, s32[]{:T(128)S(6)} %select_n.194, bf16[192,128]{1,0:T(8,128)(2,1)} %param.6), kind=kOutput, calls=%fused_computation.20 | convolution fusion | flops 201850880 | bytes 2670596 | tf_op jit(solution)/shard_map/nhl,he->nle/dot_general | solution.py:179
  7.6 2.2 %fusion.12 = bf16[32,128,128]{2,1,0:T(8,128)(2,1)S(1)} fusion(bf16[128,192,128]{2,1,0:T(8,128)(2,1)} %param.5, s32[]{:T(128)S(6)} %select_n.181, bf16[192,128]{1,0:T(8,128)(2,1)S(1)} %copy-done.2), kind=kOutput, calls=%fused_computation.19 | convolution fusion | flops 201850880 | bytes 2670596 | tf_op jit(solution)/shard_map/nhl,he->nle/dot_general | solution.py:179
  10.1 3.0 %collective-permute-start.3 = (f32[2,32,128]{2,1,0:T(8,128)S(1)}, f32[2,32,128]{2,1,0:T(8,128)S(1)}, u32[]{:S(2)}, u32[]{:S(2)}) collective-permute-start(f32[2,32,128]{2,1,0:T(8,128)S(1)} %convolution_add_fusion), channel_id=1, source_target_pairs={{0,2},{1,3},{2,0},{3,1},{4,6},{5,7},{6,4},{7,5},{8,10},{9,11},{10,... | collective-permute-start | bytes 98312 | tf_op jit(solution)/shard_map/ppermute | solution.py:101
  13.1 1.9 %collective-permute-done.3 = f32[2,32,128]{2,1,0:T(8,128)S(1)} collective-permute-done((f32[2,32,128]{2,1,0:T(8,128)S(1)}, f32[2,32,128]{2,1,0:T(8,128)S(1)}, u32[]{:S(2)}, u32[]{:S(2)}) %collective-permute-start.3) | collective-permute-done | bytes 32800 | tf_op jit(solution)/shard_map/ppermute | solution.py:101
  15.3 2.2 %convert_add_fusion.1 = f32[32,128,128]{2,1,0:T(8,128)S(1)} fusion(bf16[32,128,128]{2,1,0:T(8,128)(2,1)S(1)} %collective-permute-done, bf16[128,192,128]{2,1,0:T(8,128)(2,1)} %param.5, s32[]{:T(128)S(6)} %select_n.180, bf16[192,128]{1,0:T(8,128)(2,1)S(1)} %copy-done.2), kind=kOutput, calls=%fused_computation.8 | convolution fusion | flops 202375168 | bytes 4767748 | tf_op jit(solution)/shard_map/nhl,he->nle/dot_general | solution.py:179
  17.5 0.9 broadcast_in_dim.88
  18.4 6.4 %all-to-all-start = ((bf16[32,66,128]{2,1,0:T(8,128)(2,1)}), bf16[32,66,128]{2,1,0:T(8,128)(2,1)S(1)}, u32[]{:S(2)}, u32[]{:S(2)}) async-start(bf16[32,66,128]{2,1,0:T(8,128)(2,1)} %broadcast_in_dim.88), calls=%async_computation | async-start | bytes 1179648 | tf_op jit(solution)/shard_map/all_to_all | solution.py:140
  25.0 3.4 %add_convert_fusion = bf16[32,128,128]{2,1,0:T(8,128)(2,1)} fusion(bf16[32,128,128]{2,1,0:T(8,128)(2,1)} %collective-permute-done.4, bf16[128,192,128]{2,1,0:T(8,128)(2,1)} %param.5, s32[]{:T(128)S(6)} %select_n.193, bf16[192,128]{1,0:T(8,128)(2,1)S(1)} %copy-done.2), kind=kOutput, calls=%fused_computation.7 | convolution fusion | flops 202899456 | bytes 3719172 | tf_op jit(solution)/shard_map/nhl,he->nle/dot_general | solution.py:179
  28.4 1.8 %collective-permute-start.5 = (bf16[32,128,128]{2,1,0:T(8,128)(2,1)}, bf16[32,128,128]{2,1,0:T(8,128)(2,1)}, u32[]{:S(2)}, u32[]{:S(2)}) collective-permute-start(bf16[32,128,128]{2,1,0:T(8,128)(2,1)} %add_convert_fusion), channel_id=1, source_target_pairs={{0,2},{1,3},{2,0},{3,1},{4,6},{5,7},{6,4},{7,5},{8,10},{9,11},{10,... | collective-permute-start | bytes 3145736 | tf_op jit(solution)/shard_map/ppermute | solution.py:101
  30.2 11.3 %all-to-all-done = bf16[32,66,128]{2,1,0:T(8,128)(2,1)S(1)} async-done(((bf16[32,66,128]{2,1,0:T(8,128)(2,1)}), bf16[32,66,128]{2,1,0:T(8,128)(2,1)S(1)}, u32[]{:S(2)}, u32[]{:S(2)}) %all-to-all-start) | async-done | bytes 540704 | tf_op jit(solution)/shard_map/all_to_all | solution.py:140
  42.7 1.2 select_reduce_fusion.1
  46.0 11.4 %collective-permute-done.5 = bf16[32,128,128]{2,1,0:T(8,128)(2,1)} collective-permute-done((bf16[32,128,128]{2,1,0:T(8,128)(2,1)}, bf16[32,128,128]{2,1,0:T(8,128)(2,1)}, u32[]{:S(2)}, u32[]{:S(2)}) %collective-permute-start.5) | collective-permute-done | bytes 1048608 | tf_op jit(solution)/shard_map/ppermute | solution.py:101
  57.5 2.8 %convert_add_fusion.pre_ref = f32[32,128,128]{2,1,0:T(8,128)} fusion(f32[32,128,128]{2,1,0:T(8,128)S(1)} %convert_add_fusion.1, bf16[32,128,128]{2,1,0:T(8,128)(2,1)} %collective-permute-done.5), kind=kLoop, calls=%fused_computation.6 | loop fusion | flops 1048576 | bytes 5242880 | tf_op jit(solution)/shard_map/add | solution.py:122
  60.3 16.3 %shard_map.75 = (bf16[32,128,128]{2,1,0:T(8,128)(2,1)}, f32[256,32,128]{2,1,0:T(8,128)}, f32[256,1,128]{2,1,0:T(1,128)}) custom-call(s32[256]{0:T(256)} %reshape.271.local_ref, s32[256]{0:T(256)} %fusion.64.query_ref, f32[32,128,128]{2,1,0:T(8,128)} %convert_add_fusion.pre_ref, bf16[64,32,128]{2,1,0:T(8,128)(2,1)} %bitcast.57), custom_call_target="tpu_custom_call" | custom-call | tf_op jit(solution)/shard_map/pallas_call | solution.py:207
  76.6 1.9 %slice_reduce_fusion = f32[256]{0:T(256)S(1)} fusion(f32[256,1,128]{2,1,0:T(1,128)} %get-tuple-element.13), kind=kLoop, calls=%fused_computation.39 | loop fusion | bytes 2048 | tf_op jit(solution)/shard_map/slice | solution.py:218
  78.8 11.2 %all_to_all.20 = f32[32,1,128]{2,1,0:T(1,128)S(1)} all-to-all(f32[32,1,128]{2,1,0:T(1,128)S(1)} %reshape.278), channel_id=1, replica_groups=mesh['dp'=8,'mp'=4] {'dp','mp'}, dimensions={0} | all-to-all | bytes 32768 | tf_op jit(solution)/shard_map/all_to_all | solution.py:140
  92.0 15.6 %shard_map.76 = (bf16[64,32,128]{2,1,0:T(8,128)(2,1)}, bf16[32,128,128]{2,1,0:T(8,128)(2,1)}) custom-call(s32[256]{0:T(256)} %reshape.271.local_ref, s32[256]{0:T(256)} %fusion.64.query_ref, f32[256]{0:T(256)} %subtract_select_fusion.grad_ref, f32[32,128,128]{2,1,0:T(8,128)} %convert_add_fusion.pre_ref, bf16[32,128,128]{2,1,0:T(8,128)(2,1)} %get-tuple-element.14.emb_ref, ...), custom_call_target="tpu_custom_call" | custom-call | tf_op jit(solution)/shard_map/pallas_call | solution.py:231
  107.6 2.7 %all-to-all-start.2 = ((bf16[32,2,32,128]{3,2,1,0:T(8,128)(2,1)}), bf16[32,2,32,128]{3,2,1,0:T(8,128)(2,1)S(1)}, u32[]{:S(2)}, u32[]{:S(2)}) async-start(bf16[32,2,32,128]{3,2,1,0:T(8,128)(2,1)} %bitcast.59), calls=%async_computation.2 | async-start | bytes 1048576 | tf_op jit(solution)/shard_map/all_to_all | solution.py:140
  110.3 1.7 collective-permute-start.9
  112.0 13.9 %all-to-all-done.2 = bf16[32,2,32,128]{3,2,1,0:T(8,128)(2,1)S(1)} async-done(((bf16[32,2,32,128]{3,2,1,0:T(8,128)(2,1)}), bf16[32,2,32,128]{3,2,1,0:T(8,128)(2,1)S(1)}, u32[]{:S(2)}, u32[]{:S(2)}) %all-to-all-start.2) | async-done | bytes 524320 | tf_op jit(solution)/shard_map/all_to_all | solution.py:140
  126.2 1.3 collective-permute-start.6
  127.5 13.8 %collective-permute-done.9 = bf16[32,128,128]{2,1,0:T(8,128)(2,1)S(1)} collective-permute-done((bf16[32,128,128]{2,1,0:T(8,128)(2,1)}, bf16[32,128,128]{2,1,0:T(8,128)(2,1)S(1)}, u32[]{:S(2)}, u32[]{:S(2)}) %collective-permute-start.9) | collective-permute-done | bytes 1048608 | tf_op jit(solution)/shard_map/ppermute | solution.py:101
  142.4 1.6 collective-permute-done.7
  144.2 1.4 broadcast_select_fusion.3
  146.3 2.3 %slice-done = s8[4194304]{0:T(1024)(128)(4,1)S(1)} async-done(((s8[6291456]{0:T(1024)(128)(4,1)}), s8[4194304]{0:T(1024)(128)(4,1)S(1)}, s32[]{:S(2)}) %slice-start) | async-done | bytes 4194328
  149.3 1.8 %fusion.23 = bf16[192,128]{1,0:T(8,128)(2,1)S(1)} fusion(f32[128,192]{0,1:T(8,128)S(1)} %convolution_bitcast_fusion.1, bf16[128,192,128]{2,1,0:T(8,128)(2,1)S(1)} %bitcast.56, bf16[64,128,128]{2,1,0:T(8,128)(2,1)S(1)} %get-tuple-element.25, bf16[64,128,128]{2,1,0:T(8,128)(2,1)S(1)} %get-tuple-element.24), kind=kOutput, calls=%fused_computation.25 | convolution fusion | flops 807452672 | bytes 10633216 | tf_op jit(solution)/shard_map/nhl,nle->he/dot_general | solution.py:254
  151.9 5.6 %all-to-all-start.3 = ((bf16[8,192,128]{2,1,0:T(8,128)(2,1)}), bf16[8,192,128]{2,1,0:T(8,128)(2,1)S(1)}, u32[]{:S(2)}, u32[]{:S(2)}) async-start(bf16[8,192,128]{2,1,0:T(8,128)(2,1)} %broadcast_in_dim.100), calls=%async_computation.3 | async-start | bytes 786432 | tf_op jit(solution)/shard_map/all_to_all | solution.py:140
  157.5 0.9 fusion.34
  158.4 8.2 %convolution_bitcast_fusion = f32[128,192,128]{2,1,0:T(8,128)} fusion(bf16[64,128,128]{2,1,0:T(8,128)(2,1)} %copy-done.1, bf16[64,128,128]{2,1,0:T(8,128)(2,1)S(1)} %get-tuple-element.24, bf16[192,128]{1,0:T(8,128)(2,1)S(1)} %copy-done.2), kind=kOutput, calls=%fused_computation.1 | convolution fusion | flops 807403520 | bytes 16826368 | tf_op jit(solution)/shard_map/nle,he->nhl/dot_general | solution.py:260
  166.6 2.9 %all-to-all-done.3 = bf16[8,192,128]{2,1,0:T(8,128)(2,1)S(1)} async-done(((bf16[8,192,128]{2,1,0:T(8,128)(2,1)}), bf16[8,192,128]{2,1,0:T(8,128)(2,1)S(1)}, u32[]{:S(2)}, u32[]{:S(2)}) %all-to-all-start.3) | async-done | bytes 393248 | tf_op jit(solution)/shard_map/all_to_all | solution.py:140
  (79 shorter events, 12.8 us)
Async XLA Ops:
  0.6 0.9 copy-start
  0.6 6.9 %copy-start.2 = (bf16[192,128]{1,0:T(8,128)(2,1)S(1)}, bf16[192,128]{1,0:T(8,128)(2,1)}, u32[]{:S(2)}) copy-start(bf16[192,128]{1,0:T(8,128)(2,1)} %param.6) | copy-start | bytes 147460
  2.5 7.5 %collective-permute-start.2 = (f32[2,32,128]{2,1,0:T(8,128)S(1)}, f32[2,32,128]{2,1,0:T(8,128)S(1)}, u32[]{:S(2)}, u32[]{:S(2)}) collective-permute-start(f32[2,32,128]{2,1,0:T(8,128)S(1)} %fusion.38), channel_id=1, source_target_pairs={{0,1},{1,0},{2,3},{3,2},{4,5},{5,4},{6,7},{7,6},{8,9},{9,8},{10,11... | collective-permute-start | bytes 98312 | tf_op jit(solution)/shard_map/ppermute | solution.py:101
  3.9 9.2 %collective-permute-start.1 = (f32[2,32,128]{2,1,0:T(8,128)S(1)}, f32[2,32,128]{2,1,0:T(8,128)S(1)}, u32[]{:S(2)}, u32[]{:S(2)}) collective-permute-start(f32[2,32,128]{2,1,0:T(8,128)S(1)} %fusion.41), channel_id=1, source_target_pairs={{0,1},{1,0},{2,3},{3,2},{4,5},{5,4},{6,7},{7,6},{8,9},{9,8},{10,11... | collective-permute-start | bytes 98312 | tf_op jit(solution)/shard_map/ppermute | solution.py:101
  3.9 5.9 %copy-start.5 = (s32[2,64]{1,0:T(2,128)S(1)}, s32[2,64]{1,0:T(2,128)}, u32[]{:S(2)}) copy-start(s32[2,64]{1,0:T(2,128)} %param.7) | copy-start | bytes 1540
  7.1 17.9 %collective-permute-start.4 = (bf16[32,128,128]{2,1,0:T(8,128)(2,1)}, bf16[32,128,128]{2,1,0:T(8,128)(2,1)}, u32[]{:S(2)}, u32[]{:S(2)}) collective-permute-start(bf16[32,128,128]{2,1,0:T(8,128)(2,1)} %fusion.17), channel_id=1, source_target_pairs={{0,1},{1,0},{2,3},{3,2},{4,5},{5,4},{6,7},{7,6},{8,9},{9,8},{10,11... | collective-permute-start | bytes 3145736 | tf_op jit(solution)/shard_map/ppermute | solution.py:101
  9.8 5.5 %collective-permute-start = (bf16[32,128,128]{2,1,0:T(8,128)(2,1)S(1)}, bf16[32,128,128]{2,1,0:T(8,128)(2,1)S(1)}, u32[]{:S(2)}, u32[]{:S(2)}) collective-permute-start(bf16[32,128,128]{2,1,0:T(8,128)(2,1)S(1)} %fusion.12), channel_id=1, source_target_pairs={{0,1},{1,0},{2,3},{3,2},{4,5},{5,4},{6,7},{7,6},{8,9},{9,8},{10,11... | collective-permute-start | bytes 3145736 | tf_op jit(solution)/shard_map/ppermute | solution.py:101
  10.1 4.8 %collective-permute-start.3 = (f32[2,32,128]{2,1,0:T(8,128)S(1)}, f32[2,32,128]{2,1,0:T(8,128)S(1)}, u32[]{:S(2)}, u32[]{:S(2)}) collective-permute-start(f32[2,32,128]{2,1,0:T(8,128)S(1)} %convolution_add_fusion), channel_id=1, source_target_pairs={{0,2},{1,3},{2,0},{3,1},{4,6},{5,7},{6,4},{7,5},{8,10},{9,11},{10,... | collective-permute-start | bytes 98312 | tf_op jit(solution)/shard_map/ppermute | solution.py:101
  18.4 23.1 %all-to-all-start = ((bf16[32,66,128]{2,1,0:T(8,128)(2,1)}), bf16[32,66,128]{2,1,0:T(8,128)(2,1)S(1)}, u32[]{:S(2)}, u32[]{:S(2)}) async-start(bf16[32,66,128]{2,1,0:T(8,128)(2,1)} %broadcast_in_dim.88), calls=%async_computation | async-start | bytes 1179648 | tf_op jit(solution)/shard_map/all_to_all | solution.py:140
  28.4 29.0 %collective-permute-start.5 = (bf16[32,128,128]{2,1,0:T(8,128)(2,1)}, bf16[32,128,128]{2,1,0:T(8,128)(2,1)}, u32[]{:S(2)}, u32[]{:S(2)}) collective-permute-start(bf16[32,128,128]{2,1,0:T(8,128)(2,1)} %add_convert_fusion), channel_id=1, source_target_pairs={{0,2},{1,3},{2,0},{3,1},{4,6},{5,7},{6,4},{7,5},{8,10},{9,11},{10,... | collective-permute-start | bytes 3145736 | tf_op jit(solution)/shard_map/ppermute | solution.py:101
  60.3 18.2 %copy-start.4 = (s32[256]{0:T(256)S(1)}, s32[256]{0:T(256)}, u32[]{:S(2)}) copy-start(s32[256]{0:T(256)} %fusion.64.query_ref) | copy-start | bytes 3076
  107.6 36.7 %copy-start.3 = (bf16[32,128,128]{2,1,0:T(8,128)(2,1)S(1)}, bf16[32,128,128]{2,1,0:T(8,128)(2,1)}, u32[]{:S(2)}) copy-start(bf16[32,128,128]{2,1,0:T(8,128)(2,1)} %get-tuple-element.17) | copy-start | bytes 3145732
  107.6 18.3 %all-to-all-start.2 = ((bf16[32,2,32,128]{3,2,1,0:T(8,128)(2,1)}), bf16[32,2,32,128]{3,2,1,0:T(8,128)(2,1)S(1)}, u32[]{:S(2)}, u32[]{:S(2)}) async-start(bf16[32,2,32,128]{3,2,1,0:T(8,128)(2,1)} %bitcast.59), calls=%async_computation.2 | async-start | bytes 1048576 | tf_op jit(solution)/shard_map/all_to_all | solution.py:140
  110.3 31.0 %collective-permute-start.9 = (bf16[32,128,128]{2,1,0:T(8,128)(2,1)}, bf16[32,128,128]{2,1,0:T(8,128)(2,1)S(1)}, u32[]{:S(2)}, u32[]{:S(2)}) collective-permute-start(bf16[32,128,128]{2,1,0:T(8,128)(2,1)} %get-tuple-element.17), channel_id=1, source_target_pairs={{0,2},{1,3},{2,0},{3,1},{4,6},{5,7},{6,4},{7,5},{8,10},{9,11},{10,... | collective-permute-start | bytes 3145736 | tf_op jit(solution)/shard_map/ppermute | solution.py:101
  112.0 32.2 %collective-permute-start.11 = (bf16[32,128,128]{2,1,0:T(8,128)(2,1)}, bf16[32,128,128]{2,1,0:T(8,128)(2,1)}, u32[]{:S(2)}, u32[]{:S(2)}) collective-permute-start(bf16[32,128,128]{2,1,0:T(8,128)(2,1)} %get-tuple-element.17), channel_id=1, source_target_pairs={{0,1},{1,0},{2,3},{3,2},{4,5},{5,4},{6,7},{7,6},{8,9},{9,8},{10,11... | collective-permute-start | bytes 3145736 | tf_op jit(solution)/shard_map/ppermute | solution.py:101
  126.1 16.3 %collective-permute-start.8 = (bf16[2,32,128]{2,1,0:T(8,128)(2,1)S(1)}, bf16[2,32,128]{2,1,0:T(8,128)(2,1)S(1)}, u32[]{:S(2)}, u32[]{:S(2)}) collective-permute-start(bf16[2,32,128]{2,1,0:T(8,128)(2,1)S(1)} %fusion.28), channel_id=1, source_target_pairs={{0,1},{1,0},{2,3},{3,2},{4,5},{5,4},{6,7},{7,6},{8,9},{9,8},{10,11... | collective-permute-start | bytes 49160 | tf_op jit(solution)/shard_map/ppermute | solution.py:101
  126.2 15.7 %collective-permute-start.6 = (bf16[2,32,128]{2,1,0:T(8,128)(2,1)S(1)}, bf16[2,32,128]{2,1,0:T(8,128)(2,1)S(1)}, u32[]{:S(2)}, u32[]{:S(2)}) collective-permute-start(bf16[2,32,128]{2,1,0:T(8,128)(2,1)S(1)} %fusion.28), channel_id=1, source_target_pairs={{0,2},{1,3},{2,0},{3,1},{4,6},{5,7},{6,4},{7,5},{8,10},{9,11},{10,... | collective-permute-start | bytes 49160 | tf_op jit(solution)/shard_map/ppermute | solution.py:101
  141.3 4.3 %collective-permute-start.10 = (bf16[32,128,128]{2,1,0:T(8,128)(2,1)S(1)}, bf16[32,128,128]{2,1,0:T(8,128)(2,1)S(1)}, u32[]{:S(2)}, u32[]{:S(2)}) collective-permute-start(bf16[32,128,128]{2,1,0:T(8,128)(2,1)S(1)} %collective-permute-done.9), channel_id=1, source_target_pairs={{0,1},{1,0},{2,3},{3,2},{4,5},{5,4},{6,7},{7,6},{8,9},{9,8},{10,11... | collective-permute-start | bytes 3145736 | tf_op jit(solution)/shard_map/ppermute | solution.py:101
  141.9 2.1 %collective-permute-start.7 = (bf16[2,32,128]{2,1,0:T(8,128)(2,1)S(1)}, bf16[2,32,128]{2,1,0:T(8,128)(2,1)S(1)}, u32[]{:S(2)}, u32[]{:S(2)}) collective-permute-start(bf16[2,32,128]{2,1,0:T(8,128)(2,1)S(1)} %collective-permute-done.6), channel_id=1, source_target_pairs={{0,1},{1,0},{2,3},{3,2},{4,5},{5,4},{6,7},{7,6},{8,9},{9,8},{10,11... | collective-permute-start | bytes 49160 | tf_op jit(solution)/shard_map/ppermute | solution.py:101
  145.6 2.9 %slice-start = ((s8[6291456]{0:T(1024)(128)(4,1)}), s8[4194304]{0:T(1024)(128)(4,1)S(1)}, s32[]{:S(2)}) async-start(s8[6291456]{0:T(1024)(128)(4,1)} %bitcast.55), calls=%async_computation.4 | async-start | bytes 8388608
  145.8 3.5 %slice-start.1 = ((s8[6291456]{0:T(1024)(128)(4,1)}), s8[2097152]{0:T(1024)(128)(4,1)S(1)}, s32[]{:S(2)}) async-start(s8[6291456]{0:T(1024)(128)(4,1)} %bitcast.55), calls=%async_computation.5 | async-start | bytes 4194304
  146.3 4.8 %copy-start.1 = (bf16[64,128,128]{2,1,0:T(8,128)(2,1)}, bf16[64,128,128]{2,1,0:T(8,128)(2,1)S(1)}, u32[]{:S(2)}) copy-start(bf16[64,128,128]{2,1,0:T(8,128)(2,1)S(1)} %get-tuple-element.25) | copy-start | bytes 6291460
  151.9 17.6 %all-to-all-start.3 = ((bf16[8,192,128]{2,1,0:T(8,128)(2,1)}), bf16[8,192,128]{2,1,0:T(8,128)(2,1)S(1)}, u32[]{:S(2)}, u32[]{:S(2)}) async-start(bf16[8,192,128]{2,1,0:T(8,128)(2,1)} %broadcast_in_dim.100), calls=%async_computation.3 | async-start | bytes 786432 | tf_op jit(solution)/shard_map/all_to_all | solution.py:140
